TPU v7x, 32 devices: a whole 2x2x4 slice. The times are simulated.
32 devices in a mesh: dp: 4 (over y, x), row: 4 (over z), col: 2 (over core).
Axes of the slice: x: 2, y: 2, z: 4, core: 2. Of those that a mesh axis runs over, the one named last changes fastest.
Arguments:
- outer_gate: bfloat16 [4, 8, 1024, 1024], P('dp', None, ('row', 'col')), may hold values from -6 to 6
- inner_gate: bfloat16 [4, 8, 1024, 1024], P('dp', None, ('row', 'col')), may hold values from -6 to 6
- signal: bfloat16 [4, 8, 1024, 1024], P('dp', None, ('row', 'col')), may hold values from -6 to 6
- grad_out: bfloat16 [4, 8, 1024, 1024], P('dp', None, ('row', 'col')), may hold values from -6 to 6
- filter_weight: float32 [1024, 1024], P(('row', 'col')), may hold values from -6 to 6
Outputs:
- grad_outer: bfloat16 [4, 8, 1024, 1024], P('dp', None, ('row', 'col'))
- grad_inner: bfloat16 [4, 8, 1024, 1024], P('dp', None, ('row', 'col'))
- grad_signal: bfloat16 [4, 8, 1024, 1024], P('dp', None, ('row', 'col'))
- grad_filter: float32 [1024, 1024], P(('row', 'col'))
All inputs are finite; a program needn't handle non-finite values.
Results may differ from a plain program's by a relative error of at most 0.0013.
Values sent between devices are 32-bit elements; how exact they have to be, the bound alone decides.
No kernel may reach another device: no remote copies, remote signals or barrier semaphores. Data moves between devices by JAX's collectives and lax.ppermute only.
A program may use at most 192 MiB of HBM per device.

v0:
```python
import math

import jax
import jax.numpy as jnp
from jax import lax
from jax.sharding import PartitionSpec as P

TWO_PI = 2.0 * math.pi


def contract(form, left, right):
    return jnp.einsum(
        form, left, right, precision=lax.Precision.HIGHEST, preferred_element_type=jnp.float32
    )


def redistribute(blocks):
    return lax.all_to_all(blocks, ("row", "col"), split_axis=0, concat_axis=0, tiled=True)


def own_block():
    return lax.axis_index("row") * lax.axis_size("col") + lax.axis_index("col")


def turn_angles(first_index, second_index, total):
    product = first_index * second_index % total
    angles = product.astype(jnp.float32) * (TWO_PI / total)
    return (jnp.cos(angles), jnp.sin(angles))


def axis_dft(real, imag, sign):
    length, width = real.shape
    first = 1 << (length.bit_length() - 1) // 2
    second = length // first
    index_a = jnp.arange(first, dtype=jnp.int32)
    index_b = jnp.arange(second, dtype=jnp.int32)
    cos_a, sin_a = turn_angles(index_a[:, None], index_a[None, :], first)
    sin_a = sign * sin_a
    cos_b, sin_b = turn_angles(index_b[:, None], index_b[None, :], second)
    sin_b = sign * sin_b
    twist_cos, twist_sin = turn_angles(index_a[:, None], index_b[None, :], length)
    twist_cos = twist_cos[:, :, None]
    twist_sin = sign * twist_sin[:, :, None]
    real_three = real.reshape(first, second, width)
    step_real = contract("abm,ak->kbm", real_three, cos_a)
    step_imag = contract("abm,ak->kbm", real_three, sin_a)
    if imag is not None:
        imag_three = imag.reshape(first, second, width)
        step_real = step_real - contract("abm,ak->kbm", imag_three, sin_a)
        step_imag = step_imag + contract("abm,ak->kbm", imag_three, cos_a)
    turned_real = step_real * twist_cos - step_imag * twist_sin
    turned_imag = step_real * twist_sin + step_imag * twist_cos
    out_real = contract("kbm,bj->jkm", turned_real, cos_b) - contract(
        "kbm,bj->jkm", turned_imag, sin_b
    )
    out_imag = contract("kbm,bj->jkm", turned_real, sin_b) + contract(
        "kbm,bj->jkm", turned_imag, cos_b
    )
    return (out_real.reshape(length, width), out_imag.reshape(length, width))


def forward(stacked, order):
    count, block, grid_side = stacked.shape
    owners = grid_side // block
    total = grid_side * grid_side
    send = jnp.transpose(stacked.reshape(count, block, owners, block), (2, 1, 0, 3)).reshape(
        owners, block, count * block
    )
    columns = redistribute(send).reshape(grid_side, count * block)
    first_real, first_imag = axis_dft(columns, None, -1.0)
    first_real = first_real.reshape(grid_side, count, block)
    first_imag = first_imag.reshape(grid_side, count, block)
    col_index = own_block() * block + jnp.arange(block, dtype=jnp.int32)
    cos_turn, sin_turn = turn_angles(order[:, None, None], col_index[None, None, :], total)
    turned_real = first_real * cos_turn + first_imag * sin_turn
    turned_imag = first_imag * cos_turn - first_real * sin_turn
    send_two = jnp.concatenate([turned_real, turned_imag], axis=1).reshape(
        owners, block, 2 * count * block
    )
    gotten = redistribute(send_two).reshape(owners, block, 2 * count, block)
    flat_real = jnp.transpose(gotten[:, :, :count, :], (0, 3, 1, 2)).reshape(
        grid_side, block * count
    )
    flat_imag = jnp.transpose(gotten[:, :, count:, :], (0, 3, 1, 2)).reshape(
        grid_side, block * count
    )
    out_real, out_imag = axis_dft(flat_real, flat_imag, -1.0)
    spec_real = jnp.transpose(out_real.reshape(grid_side, block, count), (1, 2, 0))
    spec_imag = jnp.transpose(out_imag.reshape(grid_side, block, count), (1, 2, 0))
    return (spec_real, spec_imag)


def inverse(spec_real, spec_imag, order):
    block, count, grid_side = spec_real.shape
    owners = grid_side // block
    total = grid_side * grid_side
    flat_real = jnp.transpose(spec_real, (2, 0, 1)).reshape(grid_side, block * count)
    flat_imag = jnp.transpose(spec_imag, (2, 0, 1)).reshape(grid_side, block * count)
    out_real, out_imag = axis_dft(flat_real, flat_imag, 1.0)
    back_real = jnp.transpose(out_real.reshape(owners, block, block, count), (0, 2, 3, 1))
    back_imag = jnp.transpose(out_imag.reshape(owners, block, block, count), (0, 2, 3, 1))
    freq_index = lax.dynamic_slice_in_dim(order, own_block() * block, block, 0)
    col_index = (
        jnp.arange(owners, dtype=jnp.int32)[:, None] * block
        + jnp.arange(block, dtype=jnp.int32)[None, :]
    )
    cos_turn, sin_turn = turn_angles(
        freq_index[None, :, None, None], col_index[:, None, None, :], total
    )
    turned_real = back_real * cos_turn - back_imag * sin_turn
    turned_imag = back_real * sin_turn + back_imag * cos_turn
    send = jnp.concatenate([turned_real, turned_imag], axis=2).reshape(
        owners, block, 2 * count * block
    )
    gotten = redistribute(send).reshape(grid_side, 2 * count * block)
    real_part = gotten[:, : count * block]
    imag_part = gotten[:, count * block :]
    full_real, full_imag = axis_dft(real_part, imag_part, 1.0)
    values = full_real * (1.0 / total)
    returned = redistribute(values.reshape(owners, block, count * block)).reshape(
        owners, block, count, block
    )
    return jnp.transpose(returned, (2, 1, 0, 3)).reshape(count, block, grid_side)


def shards(outer_gate, inner_gate, signal, grad_out, filter_weight):
    grid_side = filter_weight.shape[1]
    freq_index = jnp.arange(grid_side, dtype=jnp.int32)
    outer_f = outer_gate[0].astype(jnp.float32)
    inner_f = inner_gate[0].astype(jnp.float32)
    signal_f = signal[0].astype(jnp.float32)
    grad_f = grad_out[0].astype(jnp.float32)
    channels = inner_f.shape[0]
    gated = inner_f * signal_f
    grad_conv = grad_f * outer_f
    taps = (filter_weight * (1.0 / grid_side))[None]
    spec_real, spec_imag = forward(jnp.concatenate([gated, grad_conv], axis=0), freq_index)
    filt_real, filt_imag = forward(taps, freq_index)
    gated_real = spec_real[:, :channels]
    gated_imag = spec_imag[:, :channels]
    cot_real = spec_real[:, channels : 2 * channels]
    cot_imag = spec_imag[:, channels : 2 * channels]
    conv_real = filt_real * gated_real - filt_imag * gated_imag
    conv_imag = filt_real * gated_imag + filt_imag * gated_real
    back_real = filt_real * cot_real + filt_imag * cot_imag
    back_imag = filt_real * cot_imag - filt_imag * cot_real
    term_real = jnp.sum(gated_real * cot_real + gated_imag * cot_imag, axis=1, keepdims=True)
    term_imag = jnp.sum(gated_real * cot_imag - gated_imag * cot_real, axis=1, keepdims=True)
    values = inverse(
        jnp.concatenate([conv_real, back_real, term_real], axis=1),
        jnp.concatenate([conv_imag, back_imag, term_imag], axis=1),
        freq_index,
    )
    grad_filter = lax.psum(values[2 * channels], "dp") * (1.0 / grid_side)
    conv = values[:channels]
    grad_gated = values[channels : 2 * channels]
    grad_outer = (grad_f * conv).astype(jnp.bfloat16)[None]
    grad_inner = (grad_gated * signal_f).astype(jnp.bfloat16)[None]
    grad_signal = (grad_gated * inner_f).astype(jnp.bfloat16)[None]
    return (grad_outer, grad_inner, grad_signal, grad_filter)


def solution(mesh):
    placed = (
        P("dp", None, ("row", "col"), None),
        P("dp", None, ("row", "col"), None),
        P("dp", None, ("row", "col"), None),
        P("dp", None, ("row", "col"), None),
        P(("row", "col"), None),
    )
    return jax.shard_map(
        shards,
        mesh=mesh,
        in_specs=placed,
        out_specs=(
            P("dp", None, ("row", "col"), None),
            P("dp", None, ("row", "col"), None),
            P("dp", None, ("row", "col"), None),
            P(("row", "col"), None),
        ),
        check_vma=False,
    )
```

profile of v0, /device:TPU:7, one launch (start us, length us, event | category | flops | bytes accessed | tf_op | source)
XLA Modules:
  0.0 2315.2 jit_solution(7356293317488337040)
XLA Ops:
  64.8 169.6 %all-to-all-done.2 = f32[8,128,2048]{1,2,0:T(8,128)} async-done(((f32[8,128,2048]{1,2,0:T(8,128)}), f32[8,128,2048]{1,2,0:T(8,128)}, u32[]{:S(2)}, u32[]{:S(2)}) %all-to-all-start.2) | async-done | bytes 8388640 | tf_op jit(solution)/shard_map/all_to_all | solution.py:18
  248.4 17.1 fusion.42
  265.5 19.1 multiply_subtract_fusion.3
  392.1 18.2 reshape.373
  410.3 17.4 copy.202
  448.1 348.3 %all-to-all-done.3 = f32[8,128,4096]{1,2,0:T(8,128)} async-done(((f32[8,128,4096]{1,2,0:T(8,128)}), f32[8,128,4096]{1,2,0:T(8,128)}, u32[]{:S(2)}, u32[]{:S(2)}) %all-to-all-start.3) | async-done | bytes 16777248 | tf_op jit(solution)/shard_map/all_to_all | solution.py:18
  816.7 20.6 reshape_reshape.63
  837.3 22.8 copy.204
  890.9 20.6 reshape_reshape.64
  911.5 22.8 copy.206
  963.9 19.3 fusion.26
  1010.3 26.6 %copy.211 = f32[32,32,2048]{1,0,2:T(8,128)} copy(f32[32,32,2048]{2,0,1:T(8,128)} %fusion.64) | data formatting | bytes 16777216 | tf_op jit(solution)/shard_map/sub | solution.py:53
  1036.9 26.1 %reshape_reshape.65 = f32[1024,128,16]{0,2,1:T(8,128)} reshape(f32[32,32,2048]{1,0,2:T(8,128)} %copy.211) | data formatting | bytes 16777216 | tf_op jit(solution)/shard_map/reshape;reshape | solution.py:88
  1063.0 18.5 fusion.67
  1081.4 26.5 %copy.218 = f32[32,32,2048]{1,0,2:T(8,128)} copy(f32[32,32,2048]{2,0,1:T(8,128)} %fusion.67) | data formatting | bytes 16777216 | tf_op jit(solution)/shard_map/add | solution.py:56
  1107.9 26.2 %reshape_reshape.67 = f32[1024,128,16]{0,2,1:T(8,128)} reshape(f32[32,32,2048]{1,0,2:T(8,128)} %copy.218) | data formatting | bytes 16777216 | tf_op jit(solution)/shard_map/reshape;reshape | solution.py:89
  1151.9 24.6 %reshape_reshape.68 = f32[32,32,2176]{1,0,2:T(8,128)} reshape(f32[1024,128,17]{0,2,1:T(8,128)} %maximum_bitcast_fusion) | data formatting | bytes 17825792 | tf_op jit(solution)/shard_map/reshape;reshape | solution.py:44
  1176.6 28.1 %copy.219 = f32[32,32,2176]{2,0,1:T(8,128)} copy(f32[32,32,2176]{1,0,2:T(8,128)} %reshape_reshape.68) | data formatting | bytes 17825792 | tf_op jit(solution)/shard_map/reshape;reshape | solution.py:44
  1233.8 24.6 %reshape_reshape.69 = f32[32,32,2176]{1,0,2:T(8,128)} reshape(f32[1024,128,17]{0,2,1:T(8,128)} %maximum_bitcast_fusion.1) | data formatting | bytes 17825792 | tf_op jit(solution)/shard_map/reshape;reshape | solution.py:48
  1258.5 28.1 %copy.220 = f32[32,32,2176]{2,0,1:T(8,128)} copy(f32[32,32,2176]{1,0,2:T(8,128)} %reshape_reshape.69) | data formatting | bytes 17825792 | tf_op jit(solution)/shard_map/reshape;reshape | solution.py:48
  1300.2 18.2 multiply_subtract_fusion.1
  1364.7 28.4 %copy.225 = f32[32,32,2176]{1,0,2:T(8,128)} copy(f32[32,32,2176]{2,0,1:T(8,128)} %fusion.44) | data formatting | bytes 17825792 | tf_op jit(solution)/shard_map/sub | solution.py:53
  1393.1 24.8 %reshape_reshape.70 = f32[8,128,128,17]{1,0,3,2:T(8,128)} reshape(f32[32,32,2176]{1,0,2:T(8,128)} %copy.225) | data formatting | bytes 17825792 | tf_op jit(solution)/shard_map/reshape;reshape | solution.py:100
  1417.8 17.3 fusion.47
  1435.1 28.0 %copy.228 = f32[32,32,2176]{1,0,2:T(8,128)} copy(f32[32,32,2176]{2,0,1:T(8,128)} %fusion.47) | data formatting | bytes 17825792 | tf_op jit(solution)/shard_map/add | solution.py:56
  1463.1 24.9 %reshape_reshape.71 = f32[8,128,128,17]{1,0,3,2:T(8,128)} reshape(f32[32,32,2176]{1,0,2:T(8,128)} %copy.228) | data formatting | bytes 17825792 | tf_op jit(solution)/shard_map/reshape;reshape | solution.py:101
  1502.1 18.5 copy.229
  1520.5 394.8 %all_to_all.30 = f32[8,128,4352]{1,2,0:T(8,128)} all-to-all(f32[8,128,4352]{1,2,0:T(8,128)} %bitcast.240), channel_id=1, replica_groups=mesh['dp'=4,'row'=4,'col'=2] {'row','col'}, dimensions={0} | all-to-all | bytes 35651584 | tf_op jit(solution)/shard_map/all_to_all | solution.py:18
  1915.3 18.0 copy.230
  1984.3 22.2 multiply_subtract_fusion
  2043.9 198.9 %all_to_all.31 = f32[8,128,2176]{2,1,0:T(8,128)} all-to-all(f32[8,128,2176]{2,1,0:T(8,128)S(1)} %bitcast.243), channel_id=1, replica_groups=mesh['dp'=4,'row'=4,'col'=2] {'row','col'}, dimensions={0} | all-to-all | bytes 17825792 | tf_op jit(solution)/shard_map/all_to_all | solution.py:18
  2285.3 20.8 all-reduce.2.cloned.1.call-done
  (177 shorter events, 560.5 us)
Async XLA Ops:
  9.2 36.6 %all-to-all-start = ((f32[8,128,128]{1,2,0:T(8,128)}), f32[8,128,128]{1,2,0:T(8,128)S(1)}, u32[]{:S(2)}, u32[]{:S(2)}) async-start(f32[8,128,128]{1,2,0:T(8,128)} %bitcast.3), calls=%async_computation | async-start | bytes 1048576 | tf_op jit(solution)/shard_map/all_to_all | solution.py:18
  29.4 12.6 copy-start.7
  45.8 188.5 %all-to-all-start.2 = ((f32[8,128,2048]{1,2,0:T(8,128)}), f32[8,128,2048]{1,2,0:T(8,128)}, u32[]{:S(2)}, u32[]{:S(2)}) async-start(f32[8,128,2048]{1,2,0:T(8,128)} %bitcast.248), calls=%async_computation.2 | async-start | bytes 16777216 | tf_op jit(solution)/shard_map/all_to_all | solution.py:18
  51.4 11.6 copy-start.19
  51.4 11.6 copy-start.23
  234.4 193.3 %all-to-all-start.1 = ((f32[8,128,256]{1,2,0:T(8,128)}), f32[8,128,256]{1,2,0:T(8,128)S(1)}, u32[]{:S(2)}, u32[]{:S(2)}) async-start(f32[8,128,256]{1,2,0:T(8,128)} %copy.180), calls=%async_computation.1 | async-start | bytes 2097152 | tf_op jit(solution)/shard_map/all_to_all | solution.py:18
  323.1 20.6 slice-start.3
  357.2 13.8 slice-start.5
  427.7 13.2 copy-start.20
  427.7 13.2 copy-start.24
  427.7 368.8 %all-to-all-start.3 = ((f32[8,128,4096]{1,2,0:T(8,128)}), f32[8,128,4096]{1,2,0:T(8,128)}, u32[]{:S(2)}, u32[]{:S(2)}) async-start(f32[8,128,4096]{1,2,0:T(8,128)} %copy.202), calls=%async_computation.3 | async-start | bytes 33554432 | tf_op jit(solution)/shard_map/all_to_all | solution.py:18
  433.6 1872.5 %all-reduce.2.cloned.1.call-start = ((), (), s32[]{:S(2)}) async-start(), calls=%async_computation.6 | async-start | bytes 1048576 | tf_op jit(solution)/shard_map/psum | solution.py:154
  860.1 11.9 copy-start.4
  963.9 32.9 %copy-start.3 = (f32[32,32,2048]{2,0,1:T(8,128)}, f32[32,32,2048]{2,0,1:T(8,128)S(1)}, u32[]{:S(2)}) copy-start(f32[32,32,2048]{2,0,1:T(8,128)S(1)} %get-tuple-element.28) | copy-start | bytes 25165828
  963.9 19.3 copy-start.5
  1107.9 26.2 %copy-start.17 = (f32[128,1,1024]{2,0,1:T(8,128)S(1)}, f32[128,1,1024]{2,0,1:T(8,128)}, u32[]{:S(2)}) copy-start(f32[128,1,1024]{2,0,1:T(8,128)} %copy.188) | copy-start | bytes 1572868
  1107.9 26.2 %copy-start.18 = (f32[128,1024]{1,0:T(8,128)S(1)}, f32[128,1024]{1,0:T(8,128)}, u32[]{:S(2)}) copy-start(f32[128,1024]{1,0:T(8,128)} %copy.215) | copy-start | bytes 1572868
  1204.7 13.2 copy-start.2
  1217.9 10.8 copy-start.11
  1217.9 10.8 copy-start.12
  1286.6 13.6 copy-start.21
  1286.6 13.6 copy-start.25
  1318.4 16.1 copy-start.1
  1318.5 30.1 %slice-start = ((s8[8912896]{0:T(1024)(128)(4,1)}), s8[4194304]{0:T(1024)(128)(4,1)S(1)}, s32[]{:S(2)}) async-start(s8[8912896]{0:T(1024)(128)(4,1)} %bitcast.231), calls=%async_computation.7 | async-start | bytes 8388608
  1318.5 30.1 %slice-start.1 = ((s8[8912896]{0:T(1024)(128)(4,1)}), s8[4194304]{0:T(1024)(128)(4,1)S(1)}, s32[]{:S(2)}) async-start(s8[8912896]{0:T(1024)(128)(4,1)} %bitcast.231), calls=%async_computation.8 | async-start | bytes 8388608
  1334.5 14.0 slice-start.2
  1463.1 24.9 %copy-start.13 = (f32[8,128,128]{2,0,1:T(8,128)S(1)}, f32[8,128,128]{2,0,1:T(8,128)}, u32[]{:S(2)}) copy-start(f32[8,128,128]{2,0,1:T(8,128)} %get-tuple-element.48) | copy-start | bytes 1572868
  1463.1 24.9 %copy-start.14 = (f32[8,128,128]{2,0,1:T(8,128)S(1)}, f32[8,128,128]{2,0,1:T(8,128)}, u32[]{:S(2)}) copy-start(f32[8,128,128]{2,0,1:T(8,128)} %get-tuple-element.49) | copy-start | bytes 1572868
  1940.1 28.0 %copy-start = (f32[1024,2176]{1,0:T(8,128)}, f32[1024,2176]{1,0:T(8,128)S(1)}, u32[]{:S(2)}) copy-start(f32[1024,2176]{1,0:T(8,128)S(1)} %get-tuple-element.20) | copy-start | bytes 26738692
  1968.0 16.2 copy-start.22
  1968.0 16.2 copy-start.26
  2006.5 14.2 copy-start.6
  (7 other events, 44.6 us)
Sparse Core Ops, SparseCore 0:
  2262.9 43.1 all-reduce.1
where the time goes:
time: 2330 us; the launch traced here: 2320 us
  local copies, waits for them, and re-layouts  626 us (27%)
  blocking collectives  594 us (25%)
  waiting for transfers between devices  539 us (23%)
  matrix products  431 us (18%)
  other arithmetic  89.2 us (4%)
    all_to_all x2, blocking collectives, redistribute(): lax.all_to_all(blocks, ('row', 'col'), split_axis=0, concat_axis=0, tiled...  594 us
    all_to_all x4, waiting for transfers between devices, redistribute(): lax.all_to_all(blocks, ('row', 'col'), split_axis=0, concat_axis=0, tiled...  518 us
    dot_general x42, matrix products, contract(): jnp.einsum(form, left, right, precision=lax.Precision.HIGHEST, preferred_...  431 us
    another operation x4, local copies, waits for them, and re-layouts, axis_dft(): imag_three = imag.reshape(first, second, width)  96.2 us
    another operation x4, local copies, waits for them, and re-layouts, axis_dft(): real_three = real.reshape(first, second, width)  96.2 us
    sub x5, local copies, waits for them, and re-layouts, axis_dft(): contract('kbm,bj->jkm', turned_real, cos_b)  67.3 us
    add x5, local copies, waits for them, and re-layouts, axis_dft(): contract('kbm,bj->jkm', turned_real, sin_b)  63.5 us
  transfers between devices with their start and end apart: 5, of which 3 were waited for; matrix products, arithmetic and copies ran while one was open for 12% of the time, Pallas kernels for 0%

commit v1 on v0

--- a/solution.py
+++ b/solution.py
@@ -1,8 +1,12 @@
+import functools
 import math
 
 import jax
 import jax.numpy as jnp
+import numpy as np
 from jax import lax
+from jax.experimental import pallas as pl
+from jax.experimental.pallas import tpu as pltpu
 from jax.sharding import PartitionSpec as P
 
 TWO_PI = 2.0 * math.pi
@@ -123,7 +127,7 @@
     return jnp.transpose(returned, (2, 1, 0, 3)).reshape(count, block, grid_side)
 
 
-def shards(outer_gate, inner_gate, signal, grad_out, filter_weight):
+def spread_shards(outer_gate, inner_gate, signal, grad_out, filter_weight):
     grid_side = filter_weight.shape[1]
     freq_index = jnp.arange(grid_side, dtype=jnp.int32)
     outer_f = outer_gate[0].astype(jnp.float32)
@@ -160,6 +164,378 @@
     return (grad_outer, grad_inner, grad_signal, grad_filter)
 
 
+VMEM_LIMIT = 40 * 1024 * 1024
+ROW_PAD = 16
+LANE_PAD = 128
+
+
+def up_to(value, unit):
+    return -(-value // unit) * unit
+
+
+def high_low(table):
+    high = table.astype(jnp.bfloat16)
+    low = (table - high.astype(np.float64)).astype(jnp.bfloat16)
+    return np.stack([high, low])
+
+
+class Plan:
+    def __init__(self, side):
+        half = side // 2
+        self.side, self.half, self.quarter = side, half, side // 4
+        self.evens = up_to(half // 2 + 1, ROW_PAD)
+        self.odds = half // 2
+        self.rows = self.evens + self.odds
+        self.even_depth = up_to(2 * self.evens, LANE_PAD)
+        total = side * side
+        even_k = 2 * np.arange(self.evens)
+        odd_k = 2 * np.arange(self.odds) + 1
+        live = (even_k <= half).astype(np.float64)
+        p = np.arange(half)
+
+        def waves(k, scale):
+            angle = 2.0 * np.pi * (k[:, None] * p[None, :] % side) / side
+            return np.concatenate([np.cos(angle) * scale[:, None], -np.sin(angle) * scale[:, None]])
+
+        ones = np.ones(self.odds)
+        self.into_even = high_low(waves(even_k, live))
+        self.into_odd = high_low(waves(odd_k, ones))
+        weight = np.where((even_k == 0) | (even_k == half), 1.0, 2.0) * live / total
+        back_even = np.zeros((half, self.even_depth))
+        back_even[:, : 2 * self.evens] = waves(even_k, weight).T
+        self.back_even = high_low(back_even)
+        self.back_odd = high_low(waves(odd_k, ones * 2.0 / total).T)
+        k = np.concatenate([even_k, odd_k])
+        turn = 2.0 * np.pi * (k[:, None] * np.arange(side)[None, :] % total) / total
+        self.turn = np.stack([np.cos(turn), np.sin(turn)]).astype(np.float32)
+        q = np.arange(self.quarter)
+        mixes = []
+        for r in range(4):
+            angle = 2.0 * np.pi * (q[:, None] * (4 * q[None, :] + r) % side) / side
+            cos, sin = np.cos(angle), np.sin(angle)
+            mixes.append(np.block([[cos, -sin], [sin, cos]]))
+        self.mix = high_low(np.stack(mixes))
+        self.row_tile = next(t for t in (176, 264, 16, 8) if self.rows % t == 0)
+
+
+def split_terms(values):
+    high = values.astype(jnp.bfloat16)
+    return high, (values - high.astype(jnp.float32)).astype(jnp.bfloat16)
+
+
+def dot_in(table, rows, high, low):
+    dot = functools.partial(jnp.dot, preferred_element_type=jnp.float32)
+    first, second = table[0, rows], table[1, rows]
+    return dot(first, high) + (dot(first, low) + dot(second, high))
+
+
+def block_views(plan, owners, me, blocks, values):
+    size = plan.side // owners
+    for step in range(owners):
+        at = pl.multiple_of((me[0] ^ step) * size, size)
+        yield blocks[step], values.at[pl.ds(at, size)]
+
+
+def tile_views(plan, grid, me, tiles, values):
+    parts, rows, cols = grid
+    height, width = plan.side // (rows * cols), plan.side // parts
+    for part in range(parts):
+        for row in range(rows):
+            for col in range(cols):
+                place = values.at[pl.ds((row * cols + col) * height, height), pl.ds(part * width, width)]
+                yield tiles[0].at[part * cols + col, row], place
+
+
+def copy_all(pairs, sems):
+    copies = [pltpu.make_async_copy(source, to, sems.at[i]) for i, (source, to) in enumerate(pairs)]
+    for copy in copies:
+        copy.start()
+    for copy in copies:
+        copy.wait()
+
+
+def forward_kernel(plan, views, count, me, *refs):
+    blocks = refs[:count]
+    into_even, into_odd, turn, mix, spec, values, mid, sems = refs[count:]
+    side, half, quarter = plan.side, plan.half, plan.quarter
+    copy_all(views(me, blocks, values), sems)
+
+    @pl.loop(0, side // quarter)
+    def columns(tile):
+        cols = pl.ds(pl.multiple_of(tile * quarter, quarter), quarter)
+        top, bottom = values[pl.ds(0, half), cols], values[pl.ds(half, half), cols]
+        for first, count, table, part in (
+            (0, plan.evens, into_even, top + bottom),
+            (plan.evens, plan.odds, into_odd, top - bottom),
+        ):
+            out = dot_in(table, slice(None), *split_terms(part))
+            real, imag = out[:count], out[count:]
+            rows = pl.ds(first, count)
+            cos, sin = turn[0, rows, cols], turn[1, rows, cols]
+            mid[0, rows, cols] = real * cos + imag * sin
+            mid[1, rows, cols] = imag * cos - real * sin
+
+    @pl.loop(0, plan.rows // plan.row_tile)
+    def rows_loop(tile):
+        rows = pl.ds(pl.multiple_of(tile * plan.row_tile, plan.row_tile), plan.row_tile)
+        real = [mid[0, rows, pl.ds(j * quarter, quarter)] for j in range(4)]
+        imag = [mid[1, rows, pl.ds(j * quarter, quarter)] for j in range(4)]
+        sum_r, sum_i = real[0] + real[2], imag[0] + imag[2]
+        dif_r, dif_i = real[0] - real[2], imag[0] - imag[2]
+        two_r, two_i = real[1] + real[3], imag[1] + imag[3]
+        odd_r, odd_i = real[1] - real[3], imag[1] - imag[3]
+        turns = (
+            (sum_r + two_r, sum_i + two_i),
+            (dif_r + odd_i, dif_i - odd_r),
+            (sum_r - two_r, sum_i - two_i),
+            (dif_r - odd_i, dif_i + odd_r),
+        )
+        dot = functools.partial(jnp.dot, preferred_element_type=jnp.float32)
+        for r, pair in enumerate(turns):
+            high, low = split_terms(jnp.concatenate(pair, axis=1))
+            out = dot(high, mix[0, r]) + (dot(low, mix[0, r]) + dot(high, mix[1, r]))
+            cols = pl.ds(r * quarter, quarter)
+            spec[0, rows, cols] = out[:, :quarter]
+            spec[1, rows, cols] = out[:, quarter:]
+
+
+def inverse_kernel(plan, views, count, conjugate, me, left, right, back_even, back_odd, turn, mix, *refs):
+    blocks = refs[:count]
+    values, mid, sems = refs[count:]
+    side, half, quarter = plan.side, plan.half, plan.quarter
+
+    @pl.loop(0, plan.rows // plan.row_tile)
+    def rows_loop(tile):
+        rows = pl.ds(pl.multiple_of(tile * plan.row_tile, plan.row_tile), plan.row_tile)
+        real, imag = [], []
+        for r in range(4):
+            cols = pl.ds(r * quarter, quarter)
+            left_r, left_i = left[0, rows, cols], left[1, rows, cols]
+            right_r, right_i = right[0, rows, cols], right[1, rows, cols]
+            if conjugate:
+                left_i = -left_i
+            pair = (left_r * right_r - left_i * right_i, left_r * right_i + left_i * right_r)
+            high, low = split_terms(jnp.concatenate(pair, axis=1))
+
+            def dot(part, table):
+                return lax.dot_general(
+                    part, table, (((1,), (1,)), ((), ())), preferred_element_type=jnp.float32
+                )
+
+            out = dot(high, mix[0, r]) + (dot(low, mix[0, r]) + dot(high, mix[1, r]))
+            real.append(out[:, :quarter])
+            imag.append(out[:, quarter:])
+        sum_r, sum_i = real[0] + real[2], imag[0] + imag[2]
+        dif_r, dif_i = real[0] - real[2], imag[0] - imag[2]
+        two_r, two_i = real[1] + real[3], imag[1] + imag[3]
+        odd_r, odd_i = real[1] - real[3], imag[1] - imag[3]
+        turns = (
+            (sum_r + two_r, sum_i + two_i),
+            (dif_r - odd_i, dif_i + odd_r),
+            (sum_r - two_r, sum_i - two_i),
+            (dif_r + odd_i, dif_i - odd_r),
+        )
+        for j, (got_r, got_i) in enumerate(turns):
+            cols = pl.ds(j * quarter, quarter)
+            cos, sin = turn[0, rows, cols], turn[1, rows, cols]
+            mid[0, rows, cols] = got_r * cos - got_i * sin
+            mid[1, rows, cols] = got_r * sin + got_i * cos
+
+    @pl.loop(0, side // quarter)
+    def columns(tile):
+        cols = pl.ds(pl.multiple_of(tile * quarter, quarter), quarter)
+        even = [mid[0, pl.ds(0, plan.evens), cols], mid[1, pl.ds(0, plan.evens), cols]]
+        if plan.even_depth > 2 * plan.evens:
+            even.append(jnp.zeros((plan.even_depth - 2 * plan.evens, quarter), jnp.float32))
+        odd = [mid[0, pl.ds(plan.evens, plan.odds), cols], mid[1, pl.ds(plan.evens, plan.odds), cols]]
+        from_even = dot_in(back_even, slice(None), *split_terms(jnp.concatenate(even)))
+        from_odd = dot_in(back_odd, slice(None), *split_terms(jnp.concatenate(odd)))
+        values[pl.ds(0, half), cols] = from_even + from_odd
+        values[pl.ds(half, half), cols] = from_even - from_odd
+
+    copy_all(((to, source) for source, to in views(me, blocks, values)), sems)
+
+
+def smem():
+    return pl.BlockSpec(memory_space=pltpu.SMEM)
+
+
+def vmem():
+    return pl.BlockSpec(memory_space=pltpu.VMEM)
+
+
+def anywhere():
+    return pl.BlockSpec(memory_space=pl.ANY)
+
+
+def kernel_cost(plan):
+    return pl.CostEstimate(flops=plan.side**2, bytes_accessed=plan.side**2, transcendentals=0)
+
+
+def to_spectrum(plan, me, blocks, views, copies):
+    count = len(blocks)
+    shape = (2, plan.rows, plan.side)
+    return pl.pallas_call(
+        functools.partial(forward_kernel, plan, views, count),
+        out_shape=jax.ShapeDtypeStruct(shape, jnp.float32),
+        in_specs=[smem()] + [anywhere()] * count + [vmem()] * 4,
+        out_specs=vmem(),
+        scratch_shapes=[
+            pltpu.VMEM((plan.side, plan.side), jnp.float32),
+            pltpu.VMEM(shape, jnp.float32),
+            pltpu.SemaphoreType.DMA((copies,)),
+        ],
+        compiler_params=pltpu.CompilerParams(vmem_limit_bytes=VMEM_LIMIT),
+        cost_estimate=kernel_cost(plan),
+        name="to_spectrum",
+    )(me, *blocks, plan.into_even, plan.into_odd, plan.turn, plan.mix)
+
+
+def from_product(plan, me, left, right, conjugate, shapes, views, copies):
+    count = len(shapes)
+    return pl.pallas_call(
+        functools.partial(inverse_kernel, plan, views, count, conjugate),
+        out_shape=[jax.ShapeDtypeStruct(shape, jnp.float32) for shape in shapes],
+        in_specs=[smem()] + [vmem()] * 6,
+        out_specs=[anywhere()] * count,
+        scratch_shapes=[
+            pltpu.VMEM((plan.side, plan.side), jnp.float32),
+            pltpu.VMEM((2, plan.rows, plan.side), jnp.float32),
+            pltpu.SemaphoreType.DMA((copies,)),
+        ],
+        compiler_params=pltpu.CompilerParams(vmem_limit_bytes=VMEM_LIMIT),
+        cost_estimate=kernel_cost(plan),
+        name="from_product",
+    )(me, left, right, plan.back_even, plan.back_odd, plan.turn, plan.mix)
+
+
+def swap(block, step, owners):
+    if step == 0:
+        return block
+    return lax.ppermute(block, ("row", "col"), [(i, i ^ step) for i in range(owners)])
+
+
+def after(first, then):
+    return lax.optimization_barrier((first, then))[1]
+
+
+def gate_kernel(owners, gates, me, *refs):
+    blocks = refs[:owners]
+    ins = refs[owners : owners + gates]
+    outs = refs[owners + gates : owners + 2 * gates]
+    got, sems = refs[owners + 2 * gates :]
+    here = pl.program_id(0)
+
+    def copy_of(step):
+        return pltpu.make_async_copy(blocks[step], got.at[step], sems.at[step])
+
+    @pl.when(here == 0)
+    def start():
+        for step in range(owners):
+            copy_of(step).start()
+
+    for step in range(owners):
+
+        @pl.when(here == step)
+        def wait():
+            copy_of(step).wait()
+
+    values = got[here]
+    for gate, out in zip(ins, outs):
+        out[0] = (gate[0].astype(jnp.float32) * values).astype(jnp.bfloat16)
+
+
+def gated_by(me, blocks, gates):
+    owners = len(blocks)
+    shape = gates[0].shape
+    spec = pl.BlockSpec((1,) + shape[1:], lambda s, me: (me[0] ^ s, 0, 0))
+    size = math.prod(shape)
+    return pl.pallas_call(
+        functools.partial(gate_kernel, owners, len(gates)),
+        grid_spec=pltpu.PrefetchScalarGridSpec(
+            num_scalar_prefetch=1,
+            grid=(owners,),
+            in_specs=[anywhere()] * owners + [spec] * len(gates),
+            out_specs=[spec] * len(gates),
+            scratch_shapes=[
+                pltpu.VMEM(shape, jnp.float32),
+                pltpu.SemaphoreType.DMA((owners,)),
+            ],
+        ),
+        out_shape=[jax.ShapeDtypeStruct(shape, jnp.bfloat16)] * len(gates),
+        compiler_params=pltpu.CompilerParams(vmem_limit_bytes=VMEM_LIMIT),
+        cost_estimate=pl.CostEstimate(
+            flops=size * len(gates), bytes_accessed=4 * size * (1 + len(gates)), transcendentals=0
+        ),
+        name="gate_out",
+    )(me, *blocks, *gates)
+
+
+def channel_shards(outer_gate, inner_gate, signal, grad_out, filter_weight):
+    side = filter_weight.shape[1]
+    block = filter_weight.shape[0]
+    plan = Plan(side)
+    parts = lax.axis_size("dp")
+    rows, cols = lax.axis_size("row"), lax.axis_size("col")
+    owners = rows * cols
+    place = own_block()
+    me = jnp.reshape(place, (1,)).astype(jnp.int32)
+    order = sorted(range(owners), key=lambda s: (-(s // cols), s % cols))
+
+    def gated_block(left, right, step):
+        at = place ^ step
+        return lax.dynamic_index_in_dim(left[0], at, 0, False).astype(
+            jnp.float32
+        ) * lax.dynamic_index_in_dim(right[0], at, 0, False).astype(jnp.float32)
+
+    width = side // parts
+    own_part = lax.dynamic_slice_in_dim(filter_weight, lax.axis_index("dp") * width, width, 1)
+    over_row = lax.all_gather(own_part * (1.0 / side), "row")
+    over_all = lax.all_gather(over_row, ("dp", "col"))
+    by_block = functools.partial(block_views, plan, owners)
+    by_tile = functools.partial(tile_views, plan, (parts, rows, cols))
+    block_shapes = [(block, side)] * owners
+    tile_shapes = [(parts * cols, rows, block, width)]
+
+    def exchange(values_of, earlier=None):
+        got = [None] * owners
+        for step in order:
+            mine = values_of(step)
+            if earlier is not None:
+                mine = after(earlier[step], mine)
+            got[step] = swap(mine, step, owners)
+        return got
+
+    gated = exchange(lambda step: gated_block(inner_gate, signal, step))
+    filt = to_spectrum(plan, me, [over_all], by_tile, parts * owners)
+    grad_conv = exchange(lambda step: gated_block(grad_out, outer_gate, step), gated)
+    gated_spec = to_spectrum(plan, me, after(filt, gated), by_block, owners)
+    conv_out = from_product(plan, me, filt, gated_spec, False, block_shapes, by_block, owners)
+    conv = exchange(lambda step: conv_out[step], grad_conv)
+    cot_spec = to_spectrum(plan, me, after(conv_out[0], grad_conv), by_block, owners)
+    back_out = from_product(plan, me, filt, cot_spec, True, block_shapes, by_block, owners)
+    grad_gated = exchange(lambda step: back_out[step], conv)
+    first = [conv[step] for step in order[:3]] + [back_out[0]]
+    (term,) = from_product(
+        plan, me, gated_spec, after(first, cot_spec), True, tile_shapes, by_tile, parts * owners
+    )
+    term = lax.psum_scatter(term, ("dp", "col"), scatter_dimension=0, tiled=False)
+    term = lax.psum_scatter(term, "row", scatter_dimension=0, tiled=False)
+    grad_filter = lax.all_gather(term * (1.0 / side), "dp", axis=1, tiled=True)
+
+    (grad_outer,) = gated_by(me, conv, [grad_out[0]])
+    grad_inner, grad_signal = gated_by(me, grad_gated, [signal[0], inner_gate[0]])
+    return (grad_outer[None], grad_inner[None], grad_signal[None], grad_filter)
+
+
+def shards(*arrays):
+    owners = lax.axis_size("row") * lax.axis_size("col")
+    side = arrays[0].shape[3]
+    whole = arrays[0].shape[1] == owners and owners & (owners - 1) == 0
+    fits = whole and side % (4 * LANE_PAD) == 0 and side % lax.axis_size("dp") == 0
+    return (channel_shards if fits else spread_shards)(*arrays)
+
+
 def solution(mesh):
     placed = (
         P("dp", None, ("row", "col"), None),

time: 2330 us -> 446 us (0.19)
  local copies, waits for them, and re-layouts: 626 us -> 28.9 us
  blocking collectives: 594 us -> 21.9 us
  matrix products: 431 us -> 0 us
  waiting for transfers between devices: 539 us -> 179 us
  Pallas kernels: 0 us -> 102 us
  other arithmetic: 89.2 us -> 7.16 us
  starting transfers between devices: 21.8 us -> 87.7 us
    all_to_all x2 -> x0, blocking collectives: 594 us -> none  [redistribute(): lax.all_to_all(blocks, ('row', 'col'), split_axis=0, concat_axis=0, tiled...]
    all_to_all x4 -> x0, waiting for transfers between devices: 518 us -> none  [redistribute(): lax.all_to_all(blocks, ('row', 'col'), split_axis=0, concat_axis=0, tiled...]
    dot_general x42 -> x0, matrix products: 431 us -> none  [contract(): jnp.einsum(form, left, right, precision=lax.Precision.HIGHEST, preferred_...]
    another operation x12 -> x0, local copies, waits for them, and re-layouts: 294 us -> none  [the longest x4 96.2 us: axis_dft(): imag_three = imag.reshape(first, second, width)]
    ppermute x0 -> x28, waiting for transfers between devices: none -> 157 us  [swap(): lax.ppermute(block, ('row', 'col'), [(i, i ^ step) for i in range(owners)])]
    pallas_call x0 -> x8, Pallas kernels: none -> 102 us  [the longest x3 52.5 us: from_product(): pl.pallas_call(functools.partial(inverse_kernel, plan, views, count, conj...]
    ppermute x0 -> x28, starting transfers between devices: none -> 87.6 us  [swap(): lax.ppermute(block, ('row', 'col'), [(i, i ^ step) for i in range(owners)])]
    sub x5 -> x0, local copies, waits for them, and re-layouts: 67.3 us -> none  [axis_dft(): contract('kbm,bj->jkm', turned_real, cos_b)]
  transfers between devices with their start and end apart: 5 -> 31, of which waited for: 3 -> 10; matrix products, arithmetic and copies ran while one was open for 12% -> 1% of each run, Pallas kernels for 0% -> 19%
where the time goes in v1:
time: 446 us; the launch traced here: 441 us
  waiting for transfers between devices  179 us (40%)
  Pallas kernels  102 us (23%)
  starting transfers between devices  87.7 us (20%)
  local copies, waits for them, and re-layouts  28.9 us (6%)
  blocking collectives  21.9 us (5%)
  between operations  14.2 us (3%)
  other arithmetic  7.16 us (2%)
    ppermute x28, waiting for transfers between devices, swap(): lax.ppermute(block, ('row', 'col'), [(i, i ^ step) for i in range(owners)])  157 us
    ppermute x28, starting transfers between devices, swap(): lax.ppermute(block, ('row', 'col'), [(i, i ^ step) for i in range(owners)])  87.6 us
    pallas_call x3, Pallas kernels, from_product(): pl.pallas_call(functools.partial(inverse_kernel, plan, views, count, conj...  52.5 us
    pallas_call x3, Pallas kernels, to_spectrum(): pl.pallas_call(functools.partial(forward_kernel, plan, views, count), out...  41.6 us
    unnamed x101, local copies, waits for them, and re-layouts  28.9 us
    reduce_scatter x1, waiting for transfers between devices, channel_shards(): lax.psum_scatter(term, ('dp', 'col'), scatter_dimension=0, tiled=False)  21.9 us
    all_gather x1, blocking collectives, channel_shards(): over_row = lax.all_gather(own_part * (1.0 / side), 'row')  14.9 us
  transfers between devices with their start and end apart: 31, of which 10 were waited for; matrix products, arithmetic and copies ran while one was open for 1% of the time, Pallas kernels for 19%

profile of v1, /device:TPU:7, one launch (start us, length us, event | category | flops | bytes accessed | tf_op | source)
XLA Modules:
  0.0 441.4 jit_solution(778529328428042268)
XLA Ops:
  8.1 14.9 %all-gather = f32[512,256]{1,0:T(8,128)} all-gather(f32[128,256]{1,0:T(8,128)S(1)} %dynamic-slice_multiply_fusion), channel_id=2, replica_groups=mesh['dp'=4,'row'=4,'col'=2] {'row'}, dimensions={0}, use_global_device_ids=true | all-gather | bytes 655360 | tf_op jit(solution)/shard_map/all_gather | solution.py:493
  23.2 3.2 multiply_bitcast_fusion.7
  28.3 4.8 %collective-permute-start.6 = (f32[128,1024]{1,0:T(8,128)S(1)}, f32[128,1024]{1,0:T(8,128)S(1)}, u32[]{:S(2)}, u32[]{:S(2)}) collective-permute-start(f32[128,1024]{1,0:T(8,128)S(1)} %get-tuple-element.130), channel_id=1, source_target_pairs={{0,7},{1,6},{2,5},{3,4},{4,3},{5,2},{6,1},{7,0},{8,15},{9,14},{10,... | collective-permute-start | bytes 1572872 | tf_op jit(solution)/shard_map/ppermute | solution.py:415
  33.1 2.5 collective-permute-start.4
  36.7 2.3 collective-permute-done.5.refs_6_
  39.8 43.7 %collective-permute-start.1 = (f32[128,1024]{1,0:T(8,128)S(1)}, f32[128,1024]{1,0:T(8,128)S(1)}, u32[]{:S(2)}, u32[]{:S(2)}) collective-permute-start(f32[128,1024]{1,0:T(8,128)S(1)} %get-tuple-element.135), channel_id=1, source_target_pairs={{0,2},{1,3},{2,0},{3,1},{4,6},{5,7},{6,4},{7,5},{8,10},{9,11},{10,... | collective-permute-start | bytes 1572872 | tf_op jit(solution)/shard_map/ppermute | solution.py:415
  83.5 10.2 %collective-permute-done.3.refs_4_ = f32[128,1024]{1,0:T(8,128)S(1)} collective-permute-done((f32[128,1024]{1,0:T(8,128)S(1)}, f32[128,1024]{1,0:T(8,128)S(1)}, u32[]{:S(2)}, u32[]{:S(2)}) %collective-permute-start.3) | collective-permute-done | bytes 524320 | tf_op jit(solution)/shard_map/ppermute | solution.py:415
  94.5 5.3 %collective-permute-start = (f32[128,1024]{1,0:T(8,128)S(1)}, f32[128,1024]{1,0:T(8,128)S(1)}, u32[]{:S(2)}, u32[]{:S(2)}) collective-permute-start(f32[128,1024]{1,0:T(8,128)S(1)} %get-tuple-element.136), channel_id=1, source_target_pairs={{0,1},{1,0},{2,3},{3,2},{4,5},{5,4},{6,7},{7,6},{8,9},{9,8},{10,11... | collective-permute-start | bytes 1572872 | tf_op jit(solution)/shard_map/ppermute | solution.py:415
  99.8 2.1 multiply_bitcast_fusion
  104.5 27.5 %collective-permute-done.4.refs_5_ = f32[128,1024]{1,0:T(8,128)S(1)} collective-permute-done((f32[128,1024]{1,0:T(8,128)S(1)}, f32[128,1024]{1,0:T(8,128)S(1)}, u32[]{:S(2)}, u32[]{:S(2)}) %collective-permute-start.4) | collective-permute-done | bytes 524320 | tf_op jit(solution)/shard_map/ppermute | solution.py:415
  139.2 2.2 copy-done
  141.4 2.2 copy-done.11
  143.6 13.7 %to_spectrum.3.left = f32[2,528,1024]{2,1,0:T(8,128)} custom-call(s32[1]{0:T(128)} %bitcast.me, f32[8,4,128,256]{3,2,1,0:T(8,128)S(1)} %bitcast.46, bf16[2,544,512]{2,1,0:T(8,128)(2,1)S(1)} %copy-done.4, bf16[2,512,512]{2,1,0:T(8,128)(2,1)S(1)} %copy-done.6, f32[2,528,1024]{2,1,0:T(8,128)} %constant.146.clone.refs_3_.refs_10_.turn, ...), custom_call_target="tpu_custom_call" | custom-call | flops 1048576 | bytes 1048576 | tf_op jit(solution)/shard_map/to_spectrum/pallas_call | solution.py:378
  157.5 13.3 %to_spectrum.4.right.left = f32[2,528,1024]{2,1,0:T(8,128)} custom-call(s32[1]{0:T(128)} %bitcast.me, f32[128,1024]{1,0:T(8,128)S(1)} %get-tuple-element.64.refs_0_, f32[128,1024]{1,0:T(8,128)S(1)} %copy-done.35, f32[128,1024]{1,0:T(8,128)S(1)} %copy-done.33, f32[128,1024]{1,0:T(8,128)S(1)} %copy-done.29, f32[128,1024]{1,0:T(8,128)S(1)} %copy-done.23, ...), custom_call_target="tpu_custom_call" | custom-call | flops 1048576 | bytes 1048576 | tf_op jit(solution)/shard_map/to_spectrum/pallas_call | solution.py:378
  170.8 2.0 collective-permute-start.9
  172.8 11.0 %collective-permute-done.13.refs_4_ = f32[128,1024]{1,0:T(8,128)} collective-permute-done((f32[128,1024]{1,0:T(8,128)}, f32[128,1024]{1,0:T(8,128)}, u32[]{:S(2)}, u32[]{:S(2)}) %collective-permute-start.13) | collective-permute-done | bytes 524320 | tf_op jit(solution)/shard_map/ppermute | solution.py:415
  183.7 5.3 %collective-permute-start.7 = (f32[128,1024]{1,0:T(8,128)S(1)}, f32[128,1024]{1,0:T(8,128)S(1)}, u32[]{:S(2)}, u32[]{:S(2)}) collective-permute-start(f32[128,1024]{1,0:T(8,128)S(1)} %copy-done.48), channel_id=1, source_target_pairs={{0,1},{1,0},{2,3},{3,2},{4,5},{5,4},{6,7},{7,6},{8,9},{9,8},{10,11... | collective-permute-start | bytes 1572872 | tf_op jit(solution)/shard_map/ppermute | solution.py:415
  189.0 17.3 %from_product.3 = (f32[128,1024]{1,0:T(8,128)S(1)}, f32[128,1024]{1,0:T(8,128)S(1)}, f32[128,1024]{1,0:T(8,128)S(1)}, f32[128,1024]{1,0:T(8,128)S(1)}, f32[128,1...) custom-call(s32[1]{0:T(128)} %bitcast.me, ...), custom_call_target="tpu_custom_call" | custom-call | flops 1048576 | bytes 1048576 | tf_op jit(solution)/shard_map/from_product/pallas_call | solution.py:396
  212.7 14.6 %to_spectrum.5.right = f32[2,528,1024]{2,1,0:T(8,128)} custom-call(s32[1]{0:T(128)} %bitcast.me, f32[128,1024]{1,0:T(8,128)S(1)} %get-tuple-element.95.refs_0_, f32[128,1024]{1,0:T(8,128)S(1)} %collective-permute-done.7.refs_1_, f32[128,1024]{1,0:T(8,128)S(1)} %collective-permute-done.9.refs_2_, f32[128,1024]{1,0:T(8,128)} %collective-permute-done.11.refs_3_, ...), custom_call_target="tpu_custom_call" | custom-call | flops 1048576 | bytes 1048576 | tf_op jit(solution)/shard_map/to_spectrum/pallas_call | solution.py:378
  227.3 17.4 %from_product.4 = (f32[128,1024]{1,0:T(8,128)S(1)}, f32[128,1024]{1,0:T(8,128)S(1)}, f32[128,1024]{1,0:T(8,128)S(1)}, f32[128,1024]{1,0:T(8,128)S(1)}, f32[128,1...) custom-call(s32[1]{0:T(128)} %bitcast.me, ...), custom_call_target="tpu_custom_call" | custom-call | flops 1048576 | bytes 1048576 | tf_op jit(solution)/shard_map/from_product/pallas_call | solution.py:396
  252.9 24.6 %collective-permute-done.14.refs_4_ = f32[128,1024]{1,0:T(8,128)S(1)} collective-permute-done((f32[128,1024]{1,0:T(8,128)S(1)}, f32[128,1024]{1,0:T(8,128)S(1)}, u32[]{:S(2)}, u32[]{:S(2)}) %collective-permute-start.14) | collective-permute-done | bytes 524320 | tf_op jit(solution)/shard_map/ppermute | solution.py:415
  278.4 17.8 %from_product.5 = f32[8,4,128,256]{3,2,1,0:T(8,128)S(1)} custom-call(s32[1]{0:T(128)} %bitcast.me, f32[2,528,1024]{2,1,0:T(8,128)} %to_spectrum.4.right.left, f32[2,528,1024]{2,1,0:T(8,128)} %to_spectrum.5.right, bf16[2,512,640]{2,1,0:T(8,128)(2,1)S(1)} %copy-done.3, bf16[2,512,512]{2,1,0:T(8,128)(2,1)S(1)} %copy-done.5, ...), custom_call_target="tpu_custom_call" | custom-call | flops 1048576 | bytes 1048576 | tf_op jit(solution)/shard_map/from_product/pallas_call | solution.py:396
  296.2 2.0 copy-done.2
  303.2 20.7 %collective-permute-done.16.refs_5_ = f32[128,1024]{1,0:T(8,128)S(1)} collective-permute-done((f32[128,1024]{1,0:T(8,128)}, f32[128,1024]{1,0:T(8,128)S(1)}, u32[]{:S(2)}, u32[]{:S(2)}) %collective-permute-start.16) | collective-permute-done | bytes 524320 | tf_op jit(solution)/shard_map/ppermute | solution.py:415
  326.5 21.9 %reduce-scatter.3.cloned.1.call-done = f32[1,4,128,256]{3,2,1,0:T(8,128)} async-done(((f32[8,4,128,256]{3,2,1,0:T(8,128)}), f32[1,4,128,256]{3,2,1,0:T(8,128)}) %reduce-scatter.3.cloned.1.call-update) | async-done | bytes 524304 | tf_op jit(solution)/shard_map/reduce_scatter | solution.py:522
  348.4 2.8 collective-permute-start.25
  351.2 6.7 %collective-permute-done.10.refs_2_ = f32[128,1024]{1,0:T(8,128)} collective-permute-done((f32[128,1024]{1,0:T(8,128)}, f32[128,1024]{1,0:T(8,128)}, u32[]{:S(2)}, u32[]{:S(2)}) %collective-permute-start.10) | collective-permute-done | bytes 524320 | tf_op jit(solution)/shard_map/ppermute | solution.py:415
  363.6 4.4 gate_out.2
  368.0 43.0 %collective-permute-done.25.refs_5_ = f32[128,1024]{1,0:T(8,128)S(1)} collective-permute-done((f32[128,1024]{1,0:T(8,128)}, f32[128,1024]{1,0:T(8,128)S(1)}, u32[]{:S(2)}, u32[]{:S(2)}) %collective-permute-start.25) | collective-permute-done | bytes 524320 | tf_op jit(solution)/shard_map/ppermute | solution.py:415
  411.0 11.2 %collective-permute-done.24.refs_4_ = f32[128,1024]{1,0:T(8,128)S(1)} collective-permute-done((f32[128,1024]{1,0:T(8,128)}, f32[128,1024]{1,0:T(8,128)S(1)}, u32[]{:S(2)}, u32[]{:S(2)}) %collective-permute-start.24) | collective-permute-done | bytes 524320 | tf_op jit(solution)/shard_map/ppermute | solution.py:415
  422.2 3.9 gate_out.3
  427.1 7.1 %all-gather.2 = f32[1,128,1024]{2,1,0:T(8,128)S(1)} all-gather(f32[1,128,256]{2,1,0:T(8,128)S(1)} %broadcast_multiply_fusion), channel_id=4, replica_groups=mesh['dp'=4,'row'=4,'col'=2] {'dp'}, dimensions={2}, use_global_device_ids=true | all-gather | bytes 655360 | tf_op jit(solution)/shard_map/all_gather | solution.py:524
  (148 shorter events, 45.9 us)
Async XLA Ops:
  7.2 132.0 %all-gather.5.cloned.1.call-start = ((), (), s32[]{:S(2)}) async-start(), calls=%async_computation.4 | async-start | bytes 4718592 | tf_op jit(solution)/shard_map/all_gather | solution.py:494
  23.0 325.4 %reduce-scatter.3.cloned.1.call-start = ((), (), s32[]{:S(2)}) async-start(), calls=%async_computation.2 | async-start | bytes 4718592 | tf_op jit(solution)/shard_map/reduce_scatter | solution.py:522
  23.1 76.7 %copy-start.7 = (bf16[1,8,128,1024]{3,2,1,0:T(8,128)(2,1)S(1)}, bf16[1,8,128,1024]{3,2,1,0:T(8,128)(2,1)}, u32[]{:S(2)}) copy-start(bf16[1,8,128,1024]{3,2,1,0:T(8,128)(2,1)} %param.14) | copy-start | bytes 6291460
  26.4 12.6 %collective-permute-start.5 = (f32[128,1024]{1,0:T(8,128)S(1)}, f32[128,1024]{1,0:T(8,128)S(1)}, u32[]{:S(2)}, u32[]{:S(2)}) collective-permute-start(f32[128,1024]{1,0:T(8,128)S(1)} %get-tuple-element.131), channel_id=1, source_target_pairs={{0,6},{1,7},{2,4},{3,5},{4,2},{5,3},{6,0},{7,1},{8,14},{9,15},{10,... | collective-permute-start | bytes 1572872 | tf_op jit(solution)/shard_map/ppermute | solution.py:415
  28.3 65.5 %collective-permute-start.3 = (f32[128,1024]{1,0:T(8,128)S(1)}, f32[128,1024]{1,0:T(8,128)S(1)}, u32[]{:S(2)}, u32[]{:S(2)}) collective-permute-start(f32[128,1024]{1,0:T(8,128)S(1)} %get-tuple-element.133), channel_id=1, source_target_pairs={{0,4},{1,5},{2,6},{3,7},{4,0},{5,1},{6,2},{7,3},{8,12},{9,13},{10,... | collective-permute-start | bytes 1572872 | tf_op jit(solution)/shard_map/ppermute | solution.py:415
  28.3 73.6 %collective-permute-start.6 = (f32[128,1024]{1,0:T(8,128)S(1)}, f32[128,1024]{1,0:T(8,128)S(1)}, u32[]{:S(2)}, u32[]{:S(2)}) collective-permute-start(f32[128,1024]{1,0:T(8,128)S(1)} %get-tuple-element.130), channel_id=1, source_target_pairs={{0,7},{1,6},{2,5},{3,4},{4,3},{5,2},{6,1},{7,0},{8,15},{9,14},{10,... | collective-permute-start | bytes 1572872 | tf_op jit(solution)/shard_map/ppermute | solution.py:415
  33.1 98.9 %collective-permute-start.4 = (f32[128,1024]{1,0:T(8,128)S(1)}, f32[128,1024]{1,0:T(8,128)S(1)}, u32[]{:S(2)}, u32[]{:S(2)}) collective-permute-start(f32[128,1024]{1,0:T(8,128)S(1)} %get-tuple-element.132), channel_id=1, source_target_pairs={{0,5},{1,4},{2,7},{3,6},{4,1},{5,0},{6,3},{7,2},{8,13},{9,12},{10,... | collective-permute-start | bytes 1572872 | tf_op jit(solution)/shard_map/ppermute | solution.py:415
  35.6 97.3 %collective-permute-start.2 = (f32[128,1024]{1,0:T(8,128)S(1)}, f32[128,1024]{1,0:T(8,128)S(1)}, u32[]{:S(2)}, u32[]{:S(2)}) collective-permute-start(f32[128,1024]{1,0:T(8,128)S(1)} %get-tuple-element.134), channel_id=1, source_target_pairs={{0,3},{1,2},{2,1},{3,0},{4,7},{5,6},{6,5},{7,4},{8,11},{9,10},{10,... | collective-permute-start | bytes 1572872 | tf_op jit(solution)/shard_map/ppermute | solution.py:415
  39.8 95.7 %collective-permute-start.1 = (f32[128,1024]{1,0:T(8,128)S(1)}, f32[128,1024]{1,0:T(8,128)S(1)}, u32[]{:S(2)}, u32[]{:S(2)}) collective-permute-start(f32[128,1024]{1,0:T(8,128)S(1)} %get-tuple-element.135), channel_id=1, source_target_pairs={{0,2},{1,3},{2,0},{3,1},{4,6},{5,7},{6,4},{7,5},{8,10},{9,11},{10,... | collective-permute-start | bytes 1572872 | tf_op jit(solution)/shard_map/ppermute | solution.py:415
  94.5 43.5 %collective-permute-start = (f32[128,1024]{1,0:T(8,128)S(1)}, f32[128,1024]{1,0:T(8,128)S(1)}, u32[]{:S(2)}, u32[]{:S(2)}) collective-permute-start(f32[128,1024]{1,0:T(8,128)S(1)} %get-tuple-element.136), channel_id=1, source_target_pairs={{0,1},{1,0},{2,3},{3,2},{4,5},{5,4},{6,7},{7,6},{8,9},{9,8},{10,11... | collective-permute-start | bytes 1572872 | tf_op jit(solution)/shard_map/ppermute | solution.py:415
  102.7 68.0 %collective-permute-start.17 = (f32[128,1024]{1,0:T(8,128)}, f32[128,1024]{1,0:T(8,128)}, u32[]{:S(2)}, u32[]{:S(2)}) collective-permute-start(f32[128,1024]{1,0:T(8,128)} %get-tuple-element.89), channel_id=1, source_target_pairs={{0,6},{1,7},{2,4},{3,5},{4,2},{5,3},{6,0},{7,1},{8,14},{9,15},{10,... | collective-permute-start | bytes 1572872 | tf_op jit(solution)/shard_map/ppermute | solution.py:415
  132.8 50.9 %collective-permute-start.13 = (f32[128,1024]{1,0:T(8,128)}, f32[128,1024]{1,0:T(8,128)}, u32[]{:S(2)}, u32[]{:S(2)}) collective-permute-start(f32[128,1024]{1,0:T(8,128)} %get-tuple-element.83), channel_id=1, source_target_pairs={{0,4},{1,5},{2,6},{3,7},{4,0},{5,1},{6,2},{7,3},{8,12},{9,13},{10,... | collective-permute-start | bytes 1572872 | tf_op jit(solution)/shard_map/ppermute | solution.py:415
  133.7 75.8 %collective-permute-start.19 = (f32[128,1024]{1,0:T(8,128)}, f32[128,1024]{1,0:T(8,128)}, u32[]{:S(2)}, u32[]{:S(2)}) collective-permute-start(f32[128,1024]{1,0:T(8,128)} %get-tuple-element.92), channel_id=1, source_target_pairs={{0,7},{1,6},{2,5},{3,4},{4,3},{5,2},{6,1},{7,0},{8,15},{9,14},{10,... | collective-permute-start | bytes 1572872 | tf_op jit(solution)/shard_map/ppermute | solution.py:415
  136.4 74.8 %collective-permute-start.15 = (f32[128,1024]{1,0:T(8,128)}, f32[128,1024]{1,0:T(8,128)}, u32[]{:S(2)}, u32[]{:S(2)}) collective-permute-start(f32[128,1024]{1,0:T(8,128)} %get-tuple-element.86), channel_id=1, source_target_pairs={{0,5},{1,4},{2,7},{3,6},{4,1},{5,0},{6,3},{7,2},{8,13},{9,12},{10,... | collective-permute-start | bytes 1572872 | tf_op jit(solution)/shard_map/ppermute | solution.py:415
  138.8 73.9 %collective-permute-start.11 = (f32[128,1024]{1,0:T(8,128)}, f32[128,1024]{1,0:T(8,128)}, u32[]{:S(2)}, u32[]{:S(2)}) collective-permute-start(f32[128,1024]{1,0:T(8,128)} %get-tuple-element.80), channel_id=1, source_target_pairs={{0,3},{1,2},{2,1},{3,0},{4,7},{5,6},{6,5},{7,4},{8,11},{9,10},{10,... | collective-permute-start | bytes 1572872 | tf_op jit(solution)/shard_map/ppermute | solution.py:415
  170.8 41.9 %collective-permute-start.9 = (f32[128,1024]{1,0:T(8,128)S(1)}, f32[128,1024]{1,0:T(8,128)S(1)}, u32[]{:S(2)}, u32[]{:S(2)}) collective-permute-start(f32[128,1024]{1,0:T(8,128)S(1)} %copy-done.49), channel_id=1, source_target_pairs={{0,2},{1,3},{2,0},{3,1},{4,6},{5,7},{6,4},{7,5},{8,10},{9,11},{10,... | collective-permute-start | bytes 1572872 | tf_op jit(solution)/shard_map/ppermute | solution.py:415
  183.7 28.9 %collective-permute-start.7 = (f32[128,1024]{1,0:T(8,128)S(1)}, f32[128,1024]{1,0:T(8,128)S(1)}, u32[]{:S(2)}, u32[]{:S(2)}) collective-permute-start(f32[128,1024]{1,0:T(8,128)S(1)} %copy-done.48), channel_id=1, source_target_pairs={{0,1},{1,0},{2,3},{3,2},{4,5},{5,4},{6,7},{7,6},{8,9},{9,8},{10,11... | collective-permute-start | bytes 1572872 | tf_op jit(solution)/shard_map/ppermute | solution.py:415
  209.5 41.8 %collective-permute-start.20 = (f32[128,1024]{1,0:T(8,128)S(1)}, f32[128,1024]{1,0:T(8,128)S(1)}, u32[]{:S(2)}, u32[]{:S(2)}) collective-permute-start(f32[128,1024]{1,0:T(8,128)S(1)} %get-tuple-element.94), channel_id=1, source_target_pairs={{0,7},{1,6},{2,5},{3,4},{4,3},{5,2},{6,1},{7,0},{8,15},{9,14},{10,... | collective-permute-start | bytes 1572872 | tf_op jit(solution)/shard_map/ppermute | solution.py:415
  211.2 40.9 %collective-permute-start.18 = (f32[128,1024]{1,0:T(8,128)S(1)}, f32[128,1024]{1,0:T(8,128)S(1)}, u32[]{:S(2)}, u32[]{:S(2)}) collective-permute-start(f32[128,1024]{1,0:T(8,128)S(1)} %get-tuple-element.91), channel_id=1, source_target_pairs={{0,6},{1,7},{2,4},{3,5},{4,2},{5,3},{6,0},{7,1},{8,14},{9,15},{10,... | collective-permute-start | bytes 1572872 | tf_op jit(solution)/shard_map/ppermute | solution.py:415
  212.7 64.9 %collective-permute-start.14 = (f32[128,1024]{1,0:T(8,128)S(1)}, f32[128,1024]{1,0:T(8,128)S(1)}, u32[]{:S(2)}, u32[]{:S(2)}) collective-permute-start(f32[128,1024]{1,0:T(8,128)S(1)} %get-tuple-element.85), channel_id=1, source_target_pairs={{0,4},{1,5},{2,6},{3,7},{4,0},{5,1},{6,2},{7,3},{8,12},{9,13},{10,... | collective-permute-start | bytes 1572872 | tf_op jit(solution)/shard_map/ppermute | solution.py:415
  298.2 127.9 %reduce-scatter.5.cloned.1.call-start = ((), (), s32[]{:S(2)}) async-start(), calls=%async_computation.3 | async-start | bytes 655360 | tf_op jit(solution)/shard_map/reduce_scatter | solution.py:523
  298.2 25.6 %collective-permute-start.16 = (f32[128,1024]{1,0:T(8,128)}, f32[128,1024]{1,0:T(8,128)S(1)}, u32[]{:S(2)}, u32[]{:S(2)}) collective-permute-start(f32[128,1024]{1,0:T(8,128)} %copy-done.45), channel_id=1, source_target_pairs={{0,5},{1,4},{2,7},{3,6},{4,1},{5,0},{6,3},{7,2},{8,13},{9,12},{10,... | collective-permute-start | bytes 1572872 | tf_op jit(solution)/shard_map/ppermute | solution.py:415
  298.5 50.0 %collective-permute-start.12 = (f32[128,1024]{1,0:T(8,128)}, f32[128,1024]{1,0:T(8,128)}, u32[]{:S(2)}, u32[]{:S(2)}) collective-permute-start(f32[128,1024]{1,0:T(8,128)} %copy-done.42), channel_id=1, source_target_pairs={{0,3},{1,2},{2,1},{3,0},{4,7},{5,6},{6,5},{7,4},{8,11},{9,10},{10,... | collective-permute-start | bytes 1572872 | tf_op jit(solution)/shard_map/ppermute | solution.py:415
  300.3 57.5 %collective-permute-start.10 = (f32[128,1024]{1,0:T(8,128)}, f32[128,1024]{1,0:T(8,128)}, u32[]{:S(2)}, u32[]{:S(2)}) collective-permute-start(f32[128,1024]{1,0:T(8,128)} %copy-done.39), channel_id=1, source_target_pairs={{0,2},{1,3},{2,0},{3,1},{4,6},{5,7},{6,4},{7,5},{8,10},{9,11},{10,... | collective-permute-start | bytes 1572872 | tf_op jit(solution)/shard_map/ppermute | solution.py:415
  301.0 56.9 %collective-permute-start.8 = (f32[128,1024]{1,0:T(8,128)}, f32[128,1024]{1,0:T(8,128)}, u32[]{:S(2)}, u32[]{:S(2)}) collective-permute-start(f32[128,1024]{1,0:T(8,128)} %copy-done.36), channel_id=1, source_target_pairs={{0,1},{1,0},{2,3},{3,2},{4,5},{5,4},{6,7},{7,6},{8,9},{9,8},{10,11... | collective-permute-start | bytes 1572872 | tf_op jit(solution)/shard_map/ppermute | solution.py:415
  301.4 58.5 %collective-permute-start.27 = (f32[128,1024]{1,0:T(8,128)}, f32[128,1024]{1,0:T(8,128)}, u32[]{:S(2)}, u32[]{:S(2)}) collective-permute-start(f32[128,1024]{1,0:T(8,128)} %copy-done.46), channel_id=1, source_target_pairs={{0,7},{1,6},{2,5},{3,4},{4,3},{5,2},{6,1},{7,0},{8,15},{9,14},{10,... | collective-permute-start | bytes 1572872 | tf_op jit(solution)/shard_map/ppermute | solution.py:415
  324.7 35.3 %collective-permute-start.26 = (f32[128,1024]{1,0:T(8,128)}, f32[128,1024]{1,0:T(8,128)}, u32[]{:S(2)}, u32[]{:S(2)}) collective-permute-start(f32[128,1024]{1,0:T(8,128)} %copy-done.44), channel_id=1, source_target_pairs={{0,6},{1,7},{2,4},{3,5},{4,2},{5,3},{6,0},{7,1},{8,14},{9,15},{10,... | collective-permute-start | bytes 1572872 | tf_op jit(solution)/shard_map/ppermute | solution.py:415
  348.4 62.5 %collective-permute-start.25 = (f32[128,1024]{1,0:T(8,128)}, f32[128,1024]{1,0:T(8,128)S(1)}, u32[]{:S(2)}, u32[]{:S(2)}) collective-permute-start(f32[128,1024]{1,0:T(8,128)} %copy-done.43), channel_id=1, source_target_pairs={{0,5},{1,4},{2,7},{3,6},{4,1},{5,0},{6,3},{7,2},{8,13},{9,12},{10,... | collective-permute-start | bytes 1572872 | tf_op jit(solution)/shard_map/ppermute | solution.py:415
  357.9 64.3 %collective-permute-start.24 = (f32[128,1024]{1,0:T(8,128)}, f32[128,1024]{1,0:T(8,128)S(1)}, u32[]{:S(2)}, u32[]{:S(2)}) collective-permute-start(f32[128,1024]{1,0:T(8,128)} %copy-done.41), channel_id=1, source_target_pairs={{0,4},{1,5},{2,6},{3,7},{4,0},{5,1},{6,2},{7,3},{8,12},{9,13},{10,... | collective-permute-start | bytes 1572872 | tf_op jit(solution)/shard_map/ppermute | solution.py:415
  357.9 64.3 %collective-permute-start.23 = (f32[128,1024]{1,0:T(8,128)}, f32[128,1024]{1,0:T(8,128)S(1)}, u32[]{:S(2)}, u32[]{:S(2)}) collective-permute-start(f32[128,1024]{1,0:T(8,128)} %copy-done.40), channel_id=1, source_target_pairs={{0,3},{1,2},{2,1},{3,0},{4,7},{5,6},{6,5},{7,4},{8,11},{9,10},{10,... | collective-permute-start | bytes 1572872 | tf_op jit(solution)/shard_map/ppermute | solution.py:415
  359.9 62.3 %collective-permute-start.22 = (f32[128,1024]{1,0:T(8,128)}, f32[128,1024]{1,0:T(8,128)S(1)}, u32[]{:S(2)}, u32[]{:S(2)}) collective-permute-start(f32[128,1024]{1,0:T(8,128)} %copy-done.38), channel_id=1, source_target_pairs={{0,2},{1,3},{2,0},{3,1},{4,6},{5,7},{6,4},{7,5},{8,10},{9,11},{10,... | collective-permute-start | bytes 1572872 | tf_op jit(solution)/shard_map/ppermute | solution.py:415
  360.0 62.2 %collective-permute-start.21 = (f32[128,1024]{1,0:T(8,128)}, f32[128,1024]{1,0:T(8,128)S(1)}, u32[]{:S(2)}, u32[]{:S(2)}) collective-permute-start(f32[128,1024]{1,0:T(8,128)} %copy-done.37), channel_id=1, source_target_pairs={{0,1},{1,0},{2,3},{3,2},{4,5},{5,4},{6,7},{7,6},{8,9},{9,8},{10,11... | collective-permute-start | bytes 1572872 | tf_op jit(solution)/shard_map/ppermute | solution.py:415
  (49 other events, 707.7 us)
Sparse Core Ops, SparseCore 0:
  23.2 39.6 all-gather.4
  298.3 50.0 reduce-scatter.2
  350.8 41.7 reduce-scatter.4

commit v2 on v1

--- a/solution.py
+++ b/solution.py
@@ -164,7 +164,8 @@
     return (grad_outer, grad_inner, grad_signal, grad_filter)
 
 
-VMEM_LIMIT = 40 * 1024 * 1024
+VMEM_LIMIT = 18 * 1024 * 1024
+UNDER_WAY = 4
 ROW_PAD = 16
 LANE_PAD = 128
 
@@ -236,29 +237,28 @@
         yield blocks[step], values.at[pl.ds(at, size)]
 
 
-def tile_views(plan, grid, me, tiles, values):
-    parts, rows, cols = grid
-    height, width = plan.side // (rows * cols), plan.side // parts
+def tile_views(plan, parts, owners, me, tiles, values):
+    height, width = plan.side // owners, plan.side // parts
     for part in range(parts):
-        for row in range(rows):
-            for col in range(cols):
-                place = values.at[pl.ds((row * cols + col) * height, height), pl.ds(part * width, width)]
-                yield tiles[0].at[part * cols + col, row], place
-
-
-def copy_all(pairs, sems):
+        for owner in range(owners):
+            place = values.at[pl.ds(owner * height, height), pl.ds(part * width, width)]
+            yield tiles[0].at[part * owners + owner], place
+
+
+def start_all(pairs, sems):
     copies = [pltpu.make_async_copy(source, to, sems.at[i]) for i, (source, to) in enumerate(pairs)]
     for copy in copies:
         copy.start()
+    return copies
+
+
+def wait_all(copies):
     for copy in copies:
         copy.wait()
 
 
-def forward_kernel(plan, views, count, me, *refs):
-    blocks = refs[:count]
-    into_even, into_odd, turn, mix, spec, values, mid, sems = refs[count:]
+def to_spectrum(plan, values, into_even, into_odd, turn, mix, spec, mid):
     side, half, quarter = plan.side, plan.half, plan.quarter
-    copy_all(views(me, blocks, values), sems)
 
     @pl.loop(0, side // quarter)
     def columns(tile):
@@ -299,10 +299,8 @@
             spec[1, rows, cols] = out[:, quarter:]
 
 
-def inverse_kernel(plan, views, count, conjugate, me, left, right, back_even, back_odd, turn, mix, *refs):
-    blocks = refs[:count]
-    values, mid, sems = refs[count:]
-    side, half, quarter = plan.side, plan.half, plan.quarter
+def inverse_rows(plan, conjugate, left, right, turn, mix, mid):
+    quarter = plan.quarter
 
     @pl.loop(0, plan.rows // plan.row_tile)
     def rows_loop(tile):
@@ -341,6 +339,10 @@
             mid[0, rows, cols] = got_r * cos - got_i * sin
             mid[1, rows, cols] = got_r * sin + got_i * cos
 
+
+def inverse_columns(plan, back_even, back_odd, mid, values):
+    side, half, quarter = plan.side, plan.half, plan.quarter
+
     @pl.loop(0, side // quarter)
     def columns(tile):
         cols = pl.ds(pl.multiple_of(tile * quarter, quarter), quarter)
@@ -353,7 +355,38 @@
         values[pl.ds(0, half), cols] = from_even + from_odd
         values[pl.ds(half, half), cols] = from_even - from_odd
 
-    copy_all(((to, source) for source, to in views(me, blocks, values)), sems)
+
+def filter_kernel(plan, views, me, tiles, into_even, into_odd, turn, mix, spec, values, mid, sems):
+    wait_all(start_all(views(me, [tiles], values), sems))
+    to_spectrum(plan, values, into_even, into_odd, turn, mix, spec, mid)
+
+
+def conv_kernel(plan, views, count, me, filt, *refs):
+    blocks, tables = refs[:count], refs[count : count + 6]
+    into_even, into_odd, back_even, back_odd, turn, mix = tables
+    spec, outs = refs[count + 6], refs[count + 7 : 2 * count + 7]
+    values, mid, sems = refs[2 * count + 7 :]
+    wait_all(start_all(views(me, blocks, values), sems))
+    to_spectrum(plan, values, into_even, into_odd, turn, mix, spec, mid)
+    inverse_rows(plan, False, filt, spec, turn, mix, mid)
+    inverse_columns(plan, back_even, back_odd, mid, values)
+    wait_all(start_all(((to, source) for source, to in views(me, outs, values)), sems))
+
+
+def grads_kernel(plan, views, term_views, count, me, filt, gated, *refs):
+    blocks, tables = refs[:count], refs[count : count + 6]
+    into_even, into_odd, back_even, back_odd, turn, mix = tables
+    outs, term = refs[count + 6 : 2 * count + 6], refs[2 * count + 6]
+    values, mid, spec, sems, term_sems = refs[2 * count + 7 :]
+    wait_all(start_all(views(me, blocks, values), sems))
+    to_spectrum(plan, values, into_even, into_odd, turn, mix, spec, mid)
+    inverse_rows(plan, True, filt, spec, turn, mix, mid)
+    inverse_columns(plan, back_even, back_odd, mid, values)
+    copies = start_all(((to, source) for source, to in views(me, outs, values)), sems)
+    inverse_rows(plan, True, gated, spec, turn, mix, mid)
+    wait_all(copies)
+    inverse_columns(plan, back_even, back_odd, mid, values)
+    wait_all(start_all(((to, source) for source, to in term_views(me, [term], values)), term_sems))
 
 
 def smem():
@@ -372,115 +405,174 @@
     return pl.CostEstimate(flops=plan.side**2, bytes_accessed=plan.side**2, transcendentals=0)
 
 
-def to_spectrum(plan, me, blocks, views, copies):
-    count = len(blocks)
+def call_kernel(plan, kernel, name, args, in_specs, out_shape, out_specs, scratch):
+    return pl.pallas_call(
+        kernel,
+        out_shape=out_shape,
+        in_specs=in_specs,
+        out_specs=out_specs,
+        scratch_shapes=scratch,
+        compiler_params=pltpu.CompilerParams(vmem_limit_bytes=VMEM_LIMIT),
+        cost_estimate=kernel_cost(plan),
+        name=name,
+    )(*args)
+
+
+def float_array(shape):
+    return jax.ShapeDtypeStruct(shape, jnp.float32)
+
+
+def filter_spectrum(plan, me, tiles, views, copies):
     shape = (2, plan.rows, plan.side)
-    return pl.pallas_call(
-        functools.partial(forward_kernel, plan, views, count),
-        out_shape=jax.ShapeDtypeStruct(shape, jnp.float32),
-        in_specs=[smem()] + [anywhere()] * count + [vmem()] * 4,
-        out_specs=vmem(),
-        scratch_shapes=[
+    return call_kernel(
+        plan,
+        functools.partial(filter_kernel, plan, views),
+        "filter_spectrum",
+        (me, tiles, plan.into_even, plan.into_odd, plan.turn, plan.mix),
+        [smem(), anywhere()] + [vmem()] * 4,
+        float_array(shape),
+        vmem(),
+        [
             pltpu.VMEM((plan.side, plan.side), jnp.float32),
             pltpu.VMEM(shape, jnp.float32),
             pltpu.SemaphoreType.DMA((copies,)),
         ],
-        compiler_params=pltpu.CompilerParams(vmem_limit_bytes=VMEM_LIMIT),
-        cost_estimate=kernel_cost(plan),
-        name="to_spectrum",
-    )(me, *blocks, plan.into_even, plan.into_odd, plan.turn, plan.mix)
-
-
-def from_product(plan, me, left, right, conjugate, shapes, views, copies):
-    count = len(shapes)
-    return pl.pallas_call(
-        functools.partial(inverse_kernel, plan, views, count, conjugate),
-        out_shape=[jax.ShapeDtypeStruct(shape, jnp.float32) for shape in shapes],
-        in_specs=[smem()] + [vmem()] * 6,
-        out_specs=[anywhere()] * count,
-        scratch_shapes=[
+    )
+
+
+def tables_of(plan):
+    return (plan.into_even, plan.into_odd, plan.back_even, plan.back_odd, plan.turn, plan.mix)
+
+
+def conv_of(plan, me, filt, blocks, views):
+    count = len(blocks)
+    shape = (2, plan.rows, plan.side)
+    spec, *outs = call_kernel(
+        plan,
+        functools.partial(conv_kernel, plan, views, count),
+        "conv_of",
+        (me, filt, *blocks, *tables_of(plan)),
+        [smem(), vmem()] + [vmem()] * count + [vmem()] * 6,
+        [float_array(shape)] + [float_array(blocks[0].shape)] * count,
+        [vmem()] * (count + 1),
+        [
             pltpu.VMEM((plan.side, plan.side), jnp.float32),
-            pltpu.VMEM((2, plan.rows, plan.side), jnp.float32),
-            pltpu.SemaphoreType.DMA((copies,)),
+            pltpu.VMEM(shape, jnp.float32),
+            pltpu.SemaphoreType.DMA((count,)),
         ],
-        compiler_params=pltpu.CompilerParams(vmem_limit_bytes=VMEM_LIMIT),
-        cost_estimate=kernel_cost(plan),
-        name="from_product",
-    )(me, left, right, plan.back_even, plan.back_odd, plan.turn, plan.mix)
-
-
-def swap(block, step, owners):
-    if step == 0:
-        return block
-    return lax.ppermute(block, ("row", "col"), [(i, i ^ step) for i in range(owners)])
+    )
+    return spec, outs
+
+
+def grads_of(plan, me, filt, gated, blocks, views, term_shape, term_views):
+    count = len(blocks)
+    shape = (2, plan.rows, plan.side)
+    *outs, term = call_kernel(
+        plan,
+        functools.partial(grads_kernel, plan, views, term_views, count),
+        "grads_of",
+        (me, filt, gated, *blocks, *tables_of(plan)),
+        [smem(), vmem(), vmem()] + [vmem()] * count + [vmem()] * 6,
+        [float_array(blocks[0].shape)] * count + [float_array(term_shape)],
+        [vmem()] * count + [anywhere()],
+        [
+            pltpu.VMEM((plan.side, plan.side), jnp.float32),
+            pltpu.VMEM(shape, jnp.float32),
+            pltpu.VMEM(shape, jnp.float32),
+            pltpu.SemaphoreType.DMA((count,)),
+            pltpu.SemaphoreType.DMA((term_shape[0],)),
+        ],
+    )
+    return outs, term
+
+
+def pairwise(block, axis, step):
+    return lax.ppermute(block, axis, [(i, i ^ step) for i in range(lax.axis_size(axis))])
 
 
 def after(first, then):
     return lax.optimization_barrier((first, then))[1]
 
 
-def gate_kernel(owners, gates, me, *refs):
-    blocks = refs[:owners]
-    ins = refs[owners : owners + gates]
-    outs = refs[owners + gates : owners + 2 * gates]
-    got, sems = refs[owners + 2 * gates :]
+def gate_kernel(steps, gates, me, *refs):
+    count = len(steps)
+    blocks = refs[:count]
+    ins = refs[count : count + gates]
+    outs, got, sems = refs[-gates - 2 : -2], refs[-2], refs[-1]
     here = pl.program_id(0)
 
-    def copy_of(step):
-        return pltpu.make_async_copy(blocks[step], got.at[step], sems.at[step])
+    def copy_of(i):
+        return pltpu.make_async_copy(blocks[i], got.at[i], sems.at[i])
 
     @pl.when(here == 0)
     def start():
-        for step in range(owners):
-            copy_of(step).start()
-
-    for step in range(owners):
-
-        @pl.when(here == step)
+        for i in range(count):
+            copy_of(i).start()
+
+    for i in range(count):
+
+        @pl.when(here == i)
         def wait():
-            copy_of(step).wait()
+            copy_of(i).wait()
 
     values = got[here]
     for gate, out in zip(ins, outs):
         out[0] = (gate[0].astype(jnp.float32) * values).astype(jnp.bfloat16)
 
 
-def gated_by(me, blocks, gates):
-    owners = len(blocks)
+def gated_by(me, steps, blocks, gates, done=()):
+    count = len(steps)
     shape = gates[0].shape
-    spec = pl.BlockSpec((1,) + shape[1:], lambda s, me: (me[0] ^ s, 0, 0))
-    size = math.prod(shape)
+
+    def place(i, me):
+        step = steps[-1]
+        for j in range(count - 1):
+            step = jnp.where(i == j, steps[j], step)
+        return (me[0] ^ step, 0, 0)
+
+    spec = pl.BlockSpec((1,) + shape[1:], place)
+    size = count * shape[1] * shape[2]
+    first_done = 1 + count + len(gates)
     return pl.pallas_call(
-        functools.partial(gate_kernel, owners, len(gates)),
+        functools.partial(gate_kernel, steps, len(gates)),
         grid_spec=pltpu.PrefetchScalarGridSpec(
             num_scalar_prefetch=1,
-            grid=(owners,),
-            in_specs=[anywhere()] * owners + [spec] * len(gates),
+            grid=(count,),
+            in_specs=[anywhere()] * count + [spec] * len(gates) + [anywhere()] * len(done),
             out_specs=[spec] * len(gates),
             scratch_shapes=[
-                pltpu.VMEM(shape, jnp.float32),
-                pltpu.SemaphoreType.DMA((owners,)),
+                pltpu.VMEM((count,) + shape[1:], jnp.float32),
+                pltpu.SemaphoreType.DMA((count,)),
             ],
         ),
         out_shape=[jax.ShapeDtypeStruct(shape, jnp.bfloat16)] * len(gates),
+        input_output_aliases={first_done + i: i for i in range(len(done))},
         compiler_params=pltpu.CompilerParams(vmem_limit_bytes=VMEM_LIMIT),
         cost_estimate=pl.CostEstimate(
             flops=size * len(gates), bytes_accessed=4 * size * (1 + len(gates)), transcendentals=0
         ),
         name="gate_out",
-    )(me, *blocks, *gates)
+    )(me, *blocks, *gates, *done)
+
+
+def send_order(owners):
+    far = sorted(range(owners // 2, owners), key=lambda s: (s & 1, -s))
+    return far + sorted(range(1, owners // 2), reverse=True)
 
 
 def channel_shards(outer_gate, inner_gate, signal, grad_out, filter_weight):
-    side = filter_weight.shape[1]
-    block = filter_weight.shape[0]
+    block, side = filter_weight.shape
     plan = Plan(side)
-    parts = lax.axis_size("dp")
-    rows, cols = lax.axis_size("row"), lax.axis_size("col")
+    parts, rows, cols = (lax.axis_size(name) for name in ("dp", "row", "col"))
     owners = rows * cols
     place = own_block()
     me = jnp.reshape(place, (1,)).astype(jnp.int32)
-    order = sorted(range(owners), key=lambda s: (-(s // cols), s % cols))
+    order = send_order(owners)
+    far = order[: owners // 2]
+    last_order = far[:-1] + order[owners // 2 :] + far[-1:]
+    width = side // parts
+    by_block = functools.partial(block_views, plan, owners)
+    by_tile = functools.partial(tile_views, plan, parts, owners)
 
     def gated_block(left, right, step):
         at = place ^ step
@@ -488,52 +580,72 @@
             jnp.float32
         ) * lax.dynamic_index_in_dim(right[0], at, 0, False).astype(jnp.float32)
 
-    width = side // parts
+    sent = []
+
+    def exchange(blocks, what, order=order):
+        got = [blocks[0]] + [None] * (owners - 1)
+        for step in order:
+            mine = blocks[step]
+            if len(sent) >= UNDER_WAY:
+                mine = after(sent[: len(sent) - UNDER_WAY + 1][-owners:], mine)
+            with jax.named_scope(f"{what}_{step}"):
+                got[step] = pairwise(mine, ("row", "col"), step)
+            sent.append(got[step])
+        return got
+
+    first = gated_block(inner_gate, signal, order[0])
+    inner_later, signal_later = after(first, [inner_gate, signal])
+    gated = exchange(
+        [
+            first if step == order[0] else gated_block(inner_later, signal_later, step)
+            for step in range(owners)
+        ],
+        "gated",
+    )
+
     own_part = lax.dynamic_slice_in_dim(filter_weight, lax.axis_index("dp") * width, width, 1)
-    over_row = lax.all_gather(own_part * (1.0 / side), "row")
-    over_all = lax.all_gather(over_row, ("dp", "col"))
-    by_block = functools.partial(block_views, plan, owners)
-    by_tile = functools.partial(tile_views, plan, (parts, rows, cols))
-    block_shapes = [(block, side)] * owners
-    tile_shapes = [(parts * cols, rows, block, width)]
-
-    def exchange(values_of, earlier=None):
-        got = [None] * owners
-        for step in order:
-            mine = values_of(step)
-            if earlier is not None:
-                mine = after(earlier[step], mine)
-            got[step] = swap(mine, step, owners)
-        return got
-
-    gated = exchange(lambda step: gated_block(inner_gate, signal, step))
-    filt = to_spectrum(plan, me, [over_all], by_tile, parts * owners)
-    grad_conv = exchange(lambda step: gated_block(grad_out, outer_gate, step), gated)
-    gated_spec = to_spectrum(plan, me, after(filt, gated), by_block, owners)
-    conv_out = from_product(plan, me, filt, gated_spec, False, block_shapes, by_block, owners)
-    conv = exchange(lambda step: conv_out[step], grad_conv)
-    cot_spec = to_spectrum(plan, me, after(conv_out[0], grad_conv), by_block, owners)
-    back_out = from_product(plan, me, filt, cot_spec, True, block_shapes, by_block, owners)
-    grad_gated = exchange(lambda step: back_out[step], conv)
-    first = [conv[step] for step in order[:3]] + [back_out[0]]
-    (term,) = from_product(
-        plan, me, gated_spec, after(first, cot_spec), True, tile_shapes, by_tile, parts * owners
-    )
-    term = lax.psum_scatter(term, ("dp", "col"), scatter_dimension=0, tiled=False)
-    term = lax.psum_scatter(term, "row", scatter_dimension=0, tiled=False)
-    grad_filter = lax.all_gather(term * (1.0 / side), "dp", axis=1, tiled=True)
-
-    (grad_outer,) = gated_by(me, conv, [grad_out[0]])
-    grad_inner, grad_signal = gated_by(me, grad_gated, [signal[0], inner_gate[0]])
+    over_all = lax.all_gather(own_part * (1.0 / side), ("dp", "row", "col"))
+    filt = filter_spectrum(plan, me, over_all, by_tile, parts * owners)
+
+    grad_conv = [gated_block(grad_out, outer_gate, step) for step in range(owners)]
+    grad_conv = exchange(grad_conv, "grad_conv")
+    spec, conv_out = conv_of(plan, me, filt, after(filt, gated), by_block)
+    conv = exchange(conv_out, "conv")
+    tile_shape = (parts * owners, block, width)
+    back_out, term = grads_of(plan, me, filt, spec, grad_conv, by_block, tile_shape, by_tile)
+    grad_gated = exchange(back_out, "grad_gated", last_order)
+
+    term = after([conv[step] for step in order[:3]], term)
+    term = lax.psum_scatter(term, ("dp", "row", "col"), scatter_dimension=0, tiled=False)
+    total = term * (1.0 / side)
+    bit = 1
+    while bit < parts:
+        other = pairwise(total, "dp", bit)
+        upper = (lax.axis_index("dp") & bit) != 0
+        total = jnp.concatenate([jnp.where(upper, other, total), jnp.where(upper, total, other)], 1)
+        bit *= 2
+    grad_filter = total
+
+    every = [0] + last_order
+    (grad_outer,) = gated_by(me, every, [conv[step] for step in every], [grad_out[0]])
+    gates = [signal[0], inner_gate[0]]
+    early, late = every[:-1], every[-1:]
+    done = gated_by(me, early, [grad_gated[step] for step in early], gates)
+    grad_inner, grad_signal = gated_by(me, late, [grad_gated[step] for step in late], gates, done)
     return (grad_outer[None], grad_inner[None], grad_signal[None], grad_filter)
 
 
+def powers_of_two(*sizes):
+    return all(size & (size - 1) == 0 for size in sizes)
+
+
 def shards(*arrays):
-    owners = lax.axis_size("row") * lax.axis_size("col")
+    parts, rows, cols = (lax.axis_size(name) for name in ("dp", "row", "col"))
     side = arrays[0].shape[3]
-    whole = arrays[0].shape[1] == owners and owners & (owners - 1) == 0
-    fits = whole and side % (4 * LANE_PAD) == 0 and side % lax.axis_size("dp") == 0
-    return (channel_shards if fits else spread_shards)(*arrays)
+    whole = arrays[0].shape[1] == rows * cols and rows * cols >= 4
+    fits = powers_of_two(parts, rows, cols, side) and side // 4 % LANE_PAD == 0
+    fits = fits and side // parts % LANE_PAD == 0
+    return (channel_shards if whole and fits else spread_shards)(*arrays)
 
 
 def solution(mesh):

time: 446 us -> 529 us (1.19)
  waiting for transfers between devices: 179 us -> 240 us
  starting transfers between devices: 87.7 us -> 148 us
  Pallas kernels: 102 us -> 78.6 us
  blocking collectives: 21.9 us -> 0 us
    reduce_scatter x2 -> x1, waiting for transfers between devices: 21.9 us -> 104 us  [channel_shards(): lax.psum_scatter(term, ('dp', 'row', 'col'), scatter_dimension=0, tiled=F...]
    ppermute x28 -> x30, starting transfers between devices: 87.6 us -> 148 us  [pairwise(): lax.ppermute(block, axis, [(i, i ^ step) for i in range(lax.axis_size(axi...]
    pallas_call x8 -> x6, Pallas kernels: 102 us -> 78.6 us  [the longest x3 69.2 us: call_kernel(): pl.pallas_call(kernel, out_shape=out_shape, in_specs=in_specs, out_specs=...]
    all_gather x2 -> x0, blocking collectives: 21.9 us -> none  [the longest x1 14.9 us: channel_shards(): over_row = lax.all_gather(own_part * (1.0 / side), 'row')]
    ppermute x28 -> x30, waiting for transfers between devices: 157 us -> 137 us  [pairwise(): lax.ppermute(block, axis, [(i, i ^ step) for i in range(lax.axis_size(axi...]
    unnamed x101 -> x124, local copies, waits for them, and re-layouts: 28.9 us -> 33.2 us
  transfers between devices with their start and end apart: 31 -> 32, of which waited for: 10 -> 11; matrix products, arithmetic and copies ran while one was open for 1% -> 2% of each run, Pallas kernels for 19% -> 15%
where the time goes in v2:
time: 529 us; the launch traced here: 526 us
  waiting for transfers between devices  240 us (45%)
  starting transfers between devices  148 us (28%)
  Pallas kernels  78.6 us (15%)
  local copies, waits for them, and re-layouts  33.2 us (6%)
  between operations  14.5 us (3%)
  other arithmetic  12.1 us (2%)
    ppermute x30, starting transfers between devices, pairwise(): lax.ppermute(block, axis, [(i, i ^ step) for i in range(lax.axis_size(axi...  148 us
    ppermute x30, waiting for transfers between devices, pairwise(): lax.ppermute(block, axis, [(i, i ^ step) for i in range(lax.axis_size(axi...  137 us
    reduce_scatter x1, waiting for transfers between devices, channel_shards(): lax.psum_scatter(term, ('dp', 'row', 'col'), scatter_dimension=0, tiled=F...  104 us
    pallas_call x3, Pallas kernels, call_kernel(): pl.pallas_call(kernel, out_shape=out_shape, in_specs=in_specs, out_specs=...  69.2 us
    unnamed x124, local copies, waits for them, and re-layouts  33.2 us
  transfers between devices with their start and end apart: 32, of which 11 were waited for; matrix products, arithmetic and copies ran while one was open for 2% of the time, Pallas kernels for 15%

profile of v2, /device:TPU:7, one launch (start us, length us, event | category | flops | bytes accessed | tf_op | source)
XLA Modules:
  0.0 526.4 jit_solution(5085421961916925966)
XLA Ops:
  10.0 3.4 collective-permute-start
  13.4 2.9 multiply_bitcast_fusion.8
  16.4 2.5 collective-permute-start.2
  19.8 5.1 collective-permute-done.refs_6_
  25.8 49.3 %collective-permute-start.5 = (f32[128,1024]{1,0:T(8,128)S(1)}, f32[128,1024]{1,0:T(8,128)S(1)}, u32[]{:S(2)}, u32[]{:S(2)}) collective-permute-start(f32[128,1024]{1,0:T(8,128)S(1)} %get-tuple-element.65), channel_id=1, source_target_pairs={{0,3},{1,2},{2,1},{3,0},{4,7},{5,6},{6,5},{7,4},{8,11},{9,10},{10,... | collective-permute-start | bytes 1572872 | tf_op jit(solution)/shard_map/gated_3/ppermute | solution.py:490
  75.0 11.2 %collective-permute-done.1.refs_4_ = f32[128,1024]{1,0:T(8,128)S(1)} collective-permute-done((f32[128,1024]{1,0:T(8,128)S(1)}, f32[128,1024]{1,0:T(8,128)S(1)}, u32[]{:S(2)}, u32[]{:S(2)}) %collective-permute-start.1) | collective-permute-done | bytes 524320 | tf_op jit(solution)/shard_map/gated_4/ppermute | solution.py:490
  89.9 2.5 collective-permute-start.3
  92.4 27.1 %collective-permute-done.6.refs_5_ = f32[128,1024]{1,0:T(8,128)S(1)} collective-permute-done((f32[128,1024]{1,0:T(8,128)S(1)}, f32[128,1024]{1,0:T(8,128)S(1)}, u32[]{:S(2)}, u32[]{:S(2)}) %collective-permute-start.6) | collective-permute-done | bytes 524320 | tf_op jit(solution)/shard_map/gated_5/ppermute | solution.py:490
  123.3 22.5 %collective-permute-done.4.refs_2_ = f32[128,1024]{1,0:T(8,128)S(1)} collective-permute-done((f32[128,1024]{1,0:T(8,128)S(1)}, f32[128,1024]{1,0:T(8,128)S(1)}, u32[]{:S(2)}, u32[]{:S(2)}) %collective-permute-start.4) | collective-permute-done | bytes 524320 | tf_op jit(solution)/shard_map/gated_2/ppermute | solution.py:490
  146.6 2.4 collective-permute-start.9
  150.6 33.9 %collective-permute-start.12 = (f32[128,1024]{1,0:T(8,128)}, f32[128,1024]{1,0:T(8,128)}, u32[]{:S(2)}, u32[]{:S(2)}) collective-permute-start(f32[128,1024]{1,0:T(8,128)} %get-tuple-element.81), channel_id=1, source_target_pairs={{0,3},{1,2},{2,1},{3,0},{4,7},{5,6},{6,5},{7,4},{8,11},{9,10},{10,... | collective-permute-start | bytes 1572872 | tf_op jit(solution)/shard_map/grad_conv_3/ppermute | solution.py:490
  184.5 5.8 %collective-permute-done.8.refs_4_ = f32[128,1024]{1,0:T(8,128)S(1)} collective-permute-done((f32[128,1024]{1,0:T(8,128)S(1)}, f32[128,1024]{1,0:T(8,128)S(1)}, u32[]{:S(2)}, u32[]{:S(2)}) %collective-permute-start.8) | collective-permute-done | bytes 524320 | tf_op jit(solution)/shard_map/grad_conv_4/ppermute | solution.py:490
  192.0 4.5 collective-permute-start.16
  196.5 2.2 copy-done
  198.7 2.2 copy-done.1
  200.9 2.2 copy-done.11
  203.2 9.9 %filter_spectrum.1.filt = f32[2,528,1024]{2,1,0:T(8,128)S(1)} custom-call(s32[1]{0:T(128)} %bitcast.me, f32[32,128,256]{2,1,0:T(8,128)S(1)} %bitcast.53, bf16[2,544,512]{2,1,0:T(8,128)(2,1)S(1)} %copy-done.4, bf16[2,512,512]{2,1,0:T(8,128)(2,1)S(1)} %copy-done.5, f32[2,528,1024]{2,1,0:T(8,128)S(1)} %copy-done, bf16[2,4,512,512]{3,2,1,0:T(8,128)(2,1)S(1)} %copy-done.1), custom_call_target="tpu_custom_call" | custom-call | flops 1048576 | bytes 1048576 | tf_op jit(solution)/shard_map/filter_spectrum/pallas_call | solution.py:409
  213.3 22.0 %conv_of.1 = (f32[2,528,1024]{2,1,0:T(8,128)S(1)}, f32[128,1024]{1,0:T(8,128)S(1)}, f32[128,1024]{1,0:T(8,128)S(1)}, f32[128,1024]{1,0:T(8,128)S(1)}, f32[128,10...) custom-call(s32[1]{0:T(128)} %bitcast.me, ...), custom_call_target="tpu_custom_call" | custom-call | flops 1048576 | bytes 1048576 | tf_op jit(solution)/shard_map/conv_of/pallas_call | solution.py:409
  238.8 10.5 %collective-permute-start.13 = (f32[128,1024]{1,0:T(8,128)S(1)}, f32[128,1024]{1,0:T(8,128)S(1)}, u32[]{:S(2)}, u32[]{:S(2)}) collective-permute-start(f32[128,1024]{1,0:T(8,128)S(1)} %get-tuple-element.83), channel_id=1, source_target_pairs={{0,4},{1,5},{2,6},{3,7},{4,0},{5,1},{6,2},{7,3},{8,12},{9,13},{10,... | collective-permute-start | bytes 1572872 | tf_op jit(solution)/shard_map/conv_4/ppermute | solution.py:490
  251.4 37.3 %grads_of.1 = (f32[128,1024]{1,0:T(8,128)S(1)}, f32[128,1024]{1,0:T(8,128)S(1)}, f32[128,1024]{1,0:T(8,128)S(1)}, f32[128,1024]{1,0:T(8,128)S(1)}, f32[128,1024]...) custom-call(s32[1]{0:T(128)} %bitcast.me, ...), custom_call_target="tpu_custom_call" | custom-call | flops 1048576 | bytes 1048576 | tf_op jit(solution)/shard_map/grads_of/pallas_call | solution.py:409
  295.6 2.7 collective-permute-done.13.refs_2_
  299.9 11.0 %collective-permute-start.20 = (f32[128,1024]{1,0:T(8,128)}, f32[128,1024]{1,0:T(8,128)S(1)}, u32[]{:S(2)}, u32[]{:S(2)}) collective-permute-start(f32[128,1024]{1,0:T(8,128)} %copy-done.58), channel_id=1, source_target_pairs={{0,5},{1,4},{2,7},{3,6},{4,1},{5,0},{6,3},{7,2},{8,13},{9,12},{10,... | collective-permute-start | bytes 1572872 | tf_op jit(solution)/shard_map/conv_5/ppermute | solution.py:490
  313.1 28.8 %collective-permute-done.20.refs_7_ = f32[128,1024]{1,0:T(8,128)S(1)} collective-permute-done((f32[128,1024]{1,0:T(8,128)}, f32[128,1024]{1,0:T(8,128)S(1)}, u32[]{:S(2)}, u32[]{:S(2)}) %collective-permute-start.20) | collective-permute-done | bytes 524320 | tf_op jit(solution)/shard_map/conv_5/ppermute | solution.py:490
  345.1 13.1 %collective-permute-done.18.refs_5_ = f32[128,1024]{1,0:T(8,128)S(1)} collective-permute-done((f32[128,1024]{1,0:T(8,128)}, f32[128,1024]{1,0:T(8,128)S(1)}, u32[]{:S(2)}, u32[]{:S(2)}) %collective-permute-start.18) | collective-permute-done | bytes 524320 | tf_op jit(solution)/shard_map/conv_2/ppermute | solution.py:490
  359.0 4.2 collective-permute-start.23
  363.2 103.6 %reduce-scatter.2.cloned.1.call-done = f32[1,128,256]{2,1,0:T(8,128)} async-done(((f32[32,128,256]{2,1,0:T(8,128)}), f32[1,128,256]{2,1,0:T(8,128)}) %reduce-scatter.2.cloned.1.call-update) | async-done | bytes 131088 | tf_op jit(solution)/shard_map/reduce_scatter | solution.py:619
  467.7 6.9 %collective-permute-start.28 = (f32[128,256]{1,0:T(8,128)S(1)}, f32[128,256]{1,0:T(8,128)S(1)}, u32[]{:S(2)}, u32[]{:S(2)}) collective-permute-start(f32[128,256]{1,0:T(8,128)S(1)} %multiply_bitcast_fusion.16), channel_id=1, source_target_pairs={{0,8},{8,0},{16,24},{24,16},{1,9},{9,1},{17,25},{25,17},{2,10},{10... | collective-permute-start | bytes 393224 | tf_op jit(solution)/shard_map/ppermute | solution.py:490
  474.7 5.7 %collective-permute-start.26 = (f32[128,1024]{1,0:T(8,128)}, f32[128,1024]{1,0:T(8,128)}, u32[]{:S(2)}, u32[]{:S(2)}) collective-permute-start(f32[128,1024]{1,0:T(8,128)} %copy-done.50), channel_id=1, source_target_pairs={{0,2},{1,3},{2,0},{3,1},{4,6},{5,7},{6,4},{7,5},{8,10},{9,11},{10,... | collective-permute-start | bytes 1572872 | tf_op jit(solution)/shard_map/grad_gated_2/ppermute | solution.py:490
  487.9 3.4 gate_out.3
  491.3 5.4 %collective-permute-done.25.refs_4_ = f32[128,1024]{1,0:T(8,128)} collective-permute-done((f32[128,1024]{1,0:T(8,128)}, f32[128,1024]{1,0:T(8,128)}, u32[]{:S(2)}, u32[]{:S(2)}) %collective-permute-start.25) | collective-permute-done | bytes 524320 | tf_op jit(solution)/shard_map/grad_gated_3/ppermute | solution.py:490
  496.8 14.8 %collective-permute-done.26.refs_5_ = f32[128,1024]{1,0:T(8,128)} collective-permute-done((f32[128,1024]{1,0:T(8,128)}, f32[128,1024]{1,0:T(8,128)}, u32[]{:S(2)}, u32[]{:S(2)}) %collective-permute-start.26) | collective-permute-done | bytes 524320 | tf_op jit(solution)/shard_map/grad_gated_2/ppermute | solution.py:490
  511.6 4.1 gate_out.4
  (174 shorter events, 48.7 us)
Async XLA Ops:
  7.2 189.3 %all-gather.3.cloned.1.call-start = ((), (), s32[]{:S(2)}) async-start(), calls=%async_computation.2 | async-start | bytes 4325376 | tf_op jit(solution)/shard_map/all_gather | solution.py:607
  8.8 458.0 %reduce-scatter.2.cloned.1.call-start = ((), (), s32[]{:S(2)}) async-start(), calls=%async_computation.1 | async-start | bytes 4325376 | tf_op jit(solution)/shard_map/reduce_scatter | solution.py:619
  10.0 15.0 %collective-permute-start = (f32[128,1024]{1,0:T(8,128)S(1)}, f32[128,1024]{1,0:T(8,128)S(1)}, u32[]{:S(2)}, u32[]{:S(2)}) collective-permute-start(f32[128,1024]{1,0:T(8,128)S(1)} %multiply_bitcast_fusion.15), channel_id=1, source_target_pairs={{0,6},{1,7},{2,4},{3,5},{4,2},{5,3},{6,0},{7,1},{8,14},{9,15},{10,... | collective-permute-start | bytes 1572872 | tf_op jit(solution)/shard_map/gated_6/ppermute | solution.py:490
  16.3 69.9 %collective-permute-start.1 = (f32[128,1024]{1,0:T(8,128)S(1)}, f32[128,1024]{1,0:T(8,128)S(1)}, u32[]{:S(2)}, u32[]{:S(2)}) collective-permute-start(f32[128,1024]{1,0:T(8,128)S(1)} %get-tuple-element.131), channel_id=1, source_target_pairs={{0,4},{1,5},{2,6},{3,7},{4,0},{5,1},{6,2},{7,3},{8,12},{9,13},{10,... | collective-permute-start | bytes 1572872 | tf_op jit(solution)/shard_map/gated_4/ppermute | solution.py:490
  16.4 72.7 %collective-permute-start.2 = (f32[128,1024]{1,0:T(8,128)S(1)}, f32[128,1024]{1,0:T(8,128)S(1)}, u32[]{:S(2)}, u32[]{:S(2)}) collective-permute-start(f32[128,1024]{1,0:T(8,128)S(1)} %get-tuple-element.130), channel_id=1, source_target_pairs={{0,7},{1,6},{2,5},{3,4},{4,3},{5,2},{6,1},{7,0},{8,15},{9,14},{10,... | collective-permute-start | bytes 1572872 | tf_op jit(solution)/shard_map/gated_7/ppermute | solution.py:490
  18.8 100.7 %collective-permute-start.6 = (f32[128,1024]{1,0:T(8,128)S(1)}, f32[128,1024]{1,0:T(8,128)S(1)}, u32[]{:S(2)}, u32[]{:S(2)}) collective-permute-start(f32[128,1024]{1,0:T(8,128)S(1)} %get-tuple-element.126), channel_id=1, source_target_pairs={{0,5},{1,4},{2,7},{3,6},{4,1},{5,0},{6,3},{7,2},{8,13},{9,12},{10,... | collective-permute-start | bytes 1572872 | tf_op jit(solution)/shard_map/gated_5/ppermute | solution.py:490
  25.8 96.8 %collective-permute-start.5 = (f32[128,1024]{1,0:T(8,128)S(1)}, f32[128,1024]{1,0:T(8,128)S(1)}, u32[]{:S(2)}, u32[]{:S(2)}) collective-permute-start(f32[128,1024]{1,0:T(8,128)S(1)} %get-tuple-element.65), channel_id=1, source_target_pairs={{0,3},{1,2},{2,1},{3,0},{4,7},{5,6},{6,5},{7,4},{8,11},{9,10},{10,... | collective-permute-start | bytes 1572872 | tf_op jit(solution)/shard_map/gated_3/ppermute | solution.py:490
  87.0 58.9 %collective-permute-start.4 = (f32[128,1024]{1,0:T(8,128)S(1)}, f32[128,1024]{1,0:T(8,128)S(1)}, u32[]{:S(2)}, u32[]{:S(2)}) collective-permute-start(f32[128,1024]{1,0:T(8,128)S(1)} %get-tuple-element.64), channel_id=1, source_target_pairs={{0,2},{1,3},{2,0},{3,1},{4,6},{5,7},{6,4},{7,5},{8,10},{9,11},{10,... | collective-permute-start | bytes 1572872 | tf_op jit(solution)/shard_map/gated_2/ppermute | solution.py:490
  89.9 59.1 %collective-permute-start.3 = (f32[128,1024]{1,0:T(8,128)S(1)}, f32[128,1024]{1,0:T(8,128)S(1)}, u32[]{:S(2)}, u32[]{:S(2)}) collective-permute-start(f32[128,1024]{1,0:T(8,128)S(1)} %get-tuple-element.63), channel_id=1, source_target_pairs={{0,1},{1,0},{2,3},{3,2},{4,5},{5,4},{6,7},{7,6},{8,9},{9,8},{10,11... | collective-permute-start | bytes 1572872 | tf_op jit(solution)/shard_map/gated_1/ppermute | solution.py:490
  120.4 29.5 %collective-permute-start.7 = (f32[128,1024]{1,0:T(8,128)S(1)}, f32[128,1024]{1,0:T(8,128)S(1)}, u32[]{:S(2)}, u32[]{:S(2)}) collective-permute-start(f32[128,1024]{1,0:T(8,128)S(1)} %get-tuple-element.75), channel_id=1, source_target_pairs={{0,6},{1,7},{2,4},{3,5},{4,2},{5,3},{6,0},{7,1},{8,14},{9,15},{10,... | collective-permute-start | bytes 1572872 | tf_op jit(solution)/shard_map/grad_conv_6/ppermute | solution.py:490
  123.3 67.0 %collective-permute-start.8 = (f32[128,1024]{1,0:T(8,128)S(1)}, f32[128,1024]{1,0:T(8,128)S(1)}, u32[]{:S(2)}, u32[]{:S(2)}) collective-permute-start(f32[128,1024]{1,0:T(8,128)S(1)} %get-tuple-element.76), channel_id=1, source_target_pairs={{0,4},{1,5},{2,6},{3,7},{4,0},{5,1},{6,2},{7,3},{8,12},{9,13},{10,... | collective-permute-start | bytes 1572872 | tf_op jit(solution)/shard_map/grad_conv_4/ppermute | solution.py:490
  146.6 44.5 %collective-permute-start.9 = (f32[128,1024]{1,0:T(8,128)S(1)}, f32[128,1024]{1,0:T(8,128)S(1)}, u32[]{:S(2)}, u32[]{:S(2)}) collective-permute-start(f32[128,1024]{1,0:T(8,128)S(1)} %get-tuple-element.77), channel_id=1, source_target_pairs={{0,7},{1,6},{2,5},{3,4},{4,3},{5,2},{6,1},{7,0},{8,15},{9,14},{10,... | collective-permute-start | bytes 1572872 | tf_op jit(solution)/shard_map/grad_conv_7/ppermute | solution.py:490
  149.8 87.9 %collective-permute-start.10 = (f32[128,1024]{1,0:T(8,128)}, f32[128,1024]{1,0:T(8,128)}, u32[]{:S(2)}, u32[]{:S(2)}) collective-permute-start(f32[128,1024]{1,0:T(8,128)} %get-tuple-element.78), channel_id=1, source_target_pairs={{0,5},{1,4},{2,7},{3,6},{4,1},{5,0},{6,3},{7,2},{8,13},{9,12},{10,... | collective-permute-start | bytes 1572872 | tf_op jit(solution)/shard_map/grad_conv_5/ppermute | solution.py:490
  150.6 88.2 %collective-permute-start.12 = (f32[128,1024]{1,0:T(8,128)}, f32[128,1024]{1,0:T(8,128)}, u32[]{:S(2)}, u32[]{:S(2)}) collective-permute-start(f32[128,1024]{1,0:T(8,128)} %get-tuple-element.81), channel_id=1, source_target_pairs={{0,3},{1,2},{2,1},{3,0},{4,7},{5,6},{6,5},{7,4},{8,11},{9,10},{10,... | collective-permute-start | bytes 1572872 | tf_op jit(solution)/shard_map/grad_conv_3/ppermute | solution.py:490
  191.1 58.1 %collective-permute-start.14 = (f32[128,1024]{1,0:T(8,128)}, f32[128,1024]{1,0:T(8,128)}, u32[]{:S(2)}, u32[]{:S(2)}) collective-permute-start(f32[128,1024]{1,0:T(8,128)} %get-tuple-element.84), channel_id=1, source_target_pairs={{0,2},{1,3},{2,0},{3,1},{4,6},{5,7},{6,4},{7,5},{8,10},{9,11},{10,... | collective-permute-start | bytes 1572872 | tf_op jit(solution)/shard_map/grad_conv_2/ppermute | solution.py:490
  192.0 59.4 %collective-permute-start.16 = (f32[128,1024]{1,0:T(8,128)}, f32[128,1024]{1,0:T(8,128)}, u32[]{:S(2)}, u32[]{:S(2)}) collective-permute-start(f32[128,1024]{1,0:T(8,128)} %get-tuple-element.87), channel_id=1, source_target_pairs={{0,1},{1,0},{2,3},{3,2},{4,5},{5,4},{6,7},{7,6},{8,9},{9,8},{10,11... | collective-permute-start | bytes 1572872 | tf_op jit(solution)/shard_map/grad_conv_1/ppermute | solution.py:490
  237.7 57.1 %collective-permute-start.11 = (f32[128,1024]{1,0:T(8,128)S(1)}, f32[128,1024]{1,0:T(8,128)S(1)}, u32[]{:S(2)}, u32[]{:S(2)}) collective-permute-start(f32[128,1024]{1,0:T(8,128)S(1)} %get-tuple-element.80), channel_id=1, source_target_pairs={{0,6},{1,7},{2,4},{3,5},{4,2},{5,3},{6,0},{7,1},{8,14},{9,15},{10,... | collective-permute-start | bytes 1572872 | tf_op jit(solution)/shard_map/conv_6/ppermute | solution.py:490
  238.8 59.5 %collective-permute-start.13 = (f32[128,1024]{1,0:T(8,128)S(1)}, f32[128,1024]{1,0:T(8,128)S(1)}, u32[]{:S(2)}, u32[]{:S(2)}) collective-permute-start(f32[128,1024]{1,0:T(8,128)S(1)} %get-tuple-element.83), channel_id=1, source_target_pairs={{0,4},{1,5},{2,6},{3,7},{4,0},{5,1},{6,2},{7,3},{8,12},{9,13},{10,... | collective-permute-start | bytes 1572872 | tf_op jit(solution)/shard_map/conv_4/ppermute | solution.py:490
  249.3 49.8 %collective-permute-start.15 = (f32[128,1024]{1,0:T(8,128)S(1)}, f32[128,1024]{1,0:T(8,128)S(1)}, u32[]{:S(2)}, u32[]{:S(2)}) collective-permute-start(f32[128,1024]{1,0:T(8,128)S(1)} %get-tuple-element.86), channel_id=1, source_target_pairs={{0,7},{1,6},{2,5},{3,4},{4,3},{5,2},{6,1},{7,0},{8,15},{9,14},{10,... | collective-permute-start | bytes 1572872 | tf_op jit(solution)/shard_map/conv_7/ppermute | solution.py:490
  299.9 42.0 %collective-permute-start.20 = (f32[128,1024]{1,0:T(8,128)}, f32[128,1024]{1,0:T(8,128)S(1)}, u32[]{:S(2)}, u32[]{:S(2)}) collective-permute-start(f32[128,1024]{1,0:T(8,128)} %copy-done.58), channel_id=1, source_target_pairs={{0,5},{1,4},{2,7},{3,6},{4,1},{5,0},{6,3},{7,2},{8,13},{9,12},{10,... | collective-permute-start | bytes 1572872 | tf_op jit(solution)/shard_map/conv_5/ppermute | solution.py:490
  310.9 33.4 %collective-permute-start.17 = (f32[128,1024]{1,0:T(8,128)}, f32[128,1024]{1,0:T(8,128)S(1)}, u32[]{:S(2)}, u32[]{:S(2)}) collective-permute-start(f32[128,1024]{1,0:T(8,128)} %copy-done.56), channel_id=1, source_target_pairs={{0,3},{1,2},{2,1},{3,0},{4,7},{5,6},{6,5},{7,4},{8,11},{9,10},{10,... | collective-permute-start | bytes 1572872 | tf_op jit(solution)/shard_map/conv_3/ppermute | solution.py:490
  311.0 47.2 %collective-permute-start.18 = (f32[128,1024]{1,0:T(8,128)}, f32[128,1024]{1,0:T(8,128)S(1)}, u32[]{:S(2)}, u32[]{:S(2)}) collective-permute-start(f32[128,1024]{1,0:T(8,128)} %copy-done.53), channel_id=1, source_target_pairs={{0,2},{1,3},{2,0},{3,1},{4,6},{5,7},{6,4},{7,5},{8,10},{9,11},{10,... | collective-permute-start | bytes 1572872 | tf_op jit(solution)/shard_map/conv_2/ppermute | solution.py:490
  312.4 162.2 %collective-permute-start.19 = (f32[128,1024]{1,0:T(8,128)}, f32[128,1024]{1,0:T(8,128)}, u32[]{:S(2)}, u32[]{:S(2)}) collective-permute-start(f32[128,1024]{1,0:T(8,128)} %copy-done.52), channel_id=1, source_target_pairs={{0,1},{1,0},{2,3},{3,2},{4,5},{5,4},{6,7},{7,6},{8,9},{9,8},{10,11... | collective-permute-start | bytes 1572872 | tf_op jit(solution)/shard_map/conv_1/ppermute | solution.py:490
  342.7 132.1 %collective-permute-start.21 = (f32[128,1024]{1,0:T(8,128)}, f32[128,1024]{1,0:T(8,128)}, u32[]{:S(2)}, u32[]{:S(2)}) collective-permute-start(f32[128,1024]{1,0:T(8,128)} %copy-done.57), channel_id=1, source_target_pairs={{0,6},{1,7},{2,4},{3,5},{4,2},{5,3},{6,0},{7,1},{8,14},{9,15},{10,... | collective-permute-start | bytes 1572872 | tf_op jit(solution)/shard_map/grad_gated_6/ppermute | solution.py:490
  345.1 135.4 %collective-permute-start.22 = (f32[128,1024]{1,0:T(8,128)}, f32[128,1024]{1,0:T(8,128)}, u32[]{:S(2)}, u32[]{:S(2)}) collective-permute-start(f32[128,1024]{1,0:T(8,128)} %copy-done.55), channel_id=1, source_target_pairs={{0,4},{1,5},{2,6},{3,7},{4,0},{5,1},{6,2},{7,3},{8,12},{9,13},{10,... | collective-permute-start | bytes 1572872 | tf_op jit(solution)/shard_map/grad_gated_4/ppermute | solution.py:490
  359.0 121.5 %collective-permute-start.23 = (f32[128,1024]{1,0:T(8,128)}, f32[128,1024]{1,0:T(8,128)}, u32[]{:S(2)}, u32[]{:S(2)}) collective-permute-start(f32[128,1024]{1,0:T(8,128)} %copy-done.54), channel_id=1, source_target_pairs={{0,7},{1,6},{2,5},{3,4},{4,3},{5,2},{6,1},{7,0},{8,15},{9,14},{10,... | collective-permute-start | bytes 1572872 | tf_op jit(solution)/shard_map/grad_gated_7/ppermute | solution.py:490
  467.7 12.9 %collective-permute-start.28 = (f32[128,256]{1,0:T(8,128)S(1)}, f32[128,256]{1,0:T(8,128)S(1)}, u32[]{:S(2)}, u32[]{:S(2)}) collective-permute-start(f32[128,256]{1,0:T(8,128)S(1)} %multiply_bitcast_fusion.16), channel_id=1, source_target_pairs={{0,8},{8,0},{16,24},{24,16},{1,9},{9,1},{17,25},{25,17},{2,10},{10... | collective-permute-start | bytes 393224 | tf_op jit(solution)/shard_map/ppermute | solution.py:490
  474.6 22.2 %collective-permute-start.25 = (f32[128,1024]{1,0:T(8,128)}, f32[128,1024]{1,0:T(8,128)}, u32[]{:S(2)}, u32[]{:S(2)}) collective-permute-start(f32[128,1024]{1,0:T(8,128)} %copy-done.51), channel_id=1, source_target_pairs={{0,3},{1,2},{2,1},{3,0},{4,7},{5,6},{6,5},{7,4},{8,11},{9,10},{10,... | collective-permute-start | bytes 1572872 | tf_op jit(solution)/shard_map/grad_gated_3/ppermute | solution.py:490
  474.7 36.9 %collective-permute-start.26 = (f32[128,1024]{1,0:T(8,128)}, f32[128,1024]{1,0:T(8,128)}, u32[]{:S(2)}, u32[]{:S(2)}) collective-permute-start(f32[128,1024]{1,0:T(8,128)} %copy-done.50), channel_id=1, source_target_pairs={{0,2},{1,3},{2,0},{3,1},{4,6},{5,7},{6,4},{7,5},{8,10},{9,11},{10,... | collective-permute-start | bytes 1572872 | tf_op jit(solution)/shard_map/grad_gated_2/ppermute | solution.py:490
  480.5 35.3 %collective-permute-start.24 = (f32[128,1024]{1,0:T(8,128)}, f32[128,1024]{1,0:T(8,128)}, u32[]{:S(2)}, u32[]{:S(2)}) collective-permute-start(f32[128,1024]{1,0:T(8,128)} %copy-done.48), channel_id=1, source_target_pairs={{0,5},{1,4},{2,7},{3,6},{4,1},{5,0},{6,3},{7,2},{8,13},{9,12},{10,... | collective-permute-start | bytes 1572872 | tf_op jit(solution)/shard_map/grad_gated_5/ppermute | solution.py:490
  480.5 31.1 %collective-permute-start.27 = (f32[128,1024]{1,0:T(8,128)}, f32[128,1024]{1,0:T(8,128)}, u32[]{:S(2)}, u32[]{:S(2)}) collective-permute-start(f32[128,1024]{1,0:T(8,128)} %copy-done.49), channel_id=1, source_target_pairs={{0,1},{1,0},{2,3},{3,2},{4,5},{5,4},{6,7},{7,6},{8,9},{9,8},{10,11... | collective-permute-start | bytes 1572872 | tf_op jit(solution)/shard_map/grad_gated_1/ppermute | solution.py:490
  482.2 35.4 %collective-permute-start.29 = (f32[128,512]{1,0:T(8,128)}, f32[128,512]{1,0:T(8,128)}, u32[]{:S(2)}, u32[]{:S(2)}) collective-permute-start(f32[128,512]{1,0:T(8,128)} %pad_maximum_fusion.1), channel_id=1, source_target_pairs={{0,16},{8,24},{16,0},{24,8},{1,17},{9,25},{17,1},{25,9},{2,18},{10... | collective-permute-start | bytes 786440 | tf_op jit(solution)/shard_map/ppermute | solution.py:490
  (62 other events, 1475.1 us)
Sparse Core Ops, SparseCore 0:
  11.0 165.3 all-gather.2
  300.0 166.6 reduce-scatter.1
